TPU v7x, 512 devices: a whole 4x4x16 slice. The times are simulated.
512 devices in a mesh: src: 16 (over z_lo, core), slab: 32 (over z_hi, x, y).
Axes of the slice: x: 4, y: 4, z: 16 (z_hi: 2, z_lo: 8; z = z_hi * 8 + z_lo), core: 2. Of those that a mesh axis runs over, the one named last changes fastest.
Arguments:
- conductivity: float32 [128, 32, 128], P('slab'), may hold values from 0.2 to 5
- forward_fields: float32 [16, 128, 32, 128], P('src', 'slab'), may hold values from -6 to 6
- receiver_pairs: int32 [16, 2000, 2], P('src'), may hold values from 0 to 524287
- observed: float32 [16, 2000], replicated, may hold values from -12 to 12
Outputs:
- gradient: float32 [128, 32, 128], P('slab', 'src')
- misfit: float32 [], replicated
All inputs are finite; a program needn't handle non-finite values.
Results may differ from a plain program's by a relative error of at most 0.0003.
Values sent between devices are 32-bit elements; how exact they have to be, the bound alone decides.
A program may use at most 64 MiB of HBM per device.

v0:
```python
import jax
import jax.numpy as jnp
from jax import lax
from jax.sharding import PartitionSpec as P

DEG = 2


LOWER = 0.3
UPPER = 2.0
OMEGA = 0.6
MASS = (1.0 / 3.0, 1.0 / 6.0, 1.0 / 6.0, 1.0 / 3.0)
STIFF = (1.0, -1.0, -1.0, 1.0)


def shifted(array, axis, by):
    count = lax.axis_size(axis)
    pairs = [(i, i + by) for i in range(count) if 0 <= i + by < count]
    return lax.ppermute(array, axis, pairs)


def with_halo(block, sides, width):
    for axis, dim in sides:
        count = lax.axis_size(axis)
        forward = [(i, i + 1) for i in range(count - 1)]
        backward = [(target, source) for source, target in forward]
        low = lax.ppermute(
            lax.slice_in_dim(block, block.shape[dim] - width, None, axis=dim), axis, forward
        )
        high = lax.ppermute(lax.slice_in_dim(block, 0, width, axis=dim), axis, backward)
        block = jnp.concatenate([low, block, high], axis=dim)
    return block


def mix_pair(matrix, lead, trail):
    return (matrix[0] * lead + matrix[1] * trail, matrix[2] * lead + matrix[3] * trail)


def along_axis(matrix, arrays, stride):
    result = list(arrays)
    for corner in range(8):
        if corner // stride % 2 == 0:
            result[corner], result[corner + stride] = mix_pair(
                matrix, arrays[corner], arrays[corner + stride]
            )
    return result


def element_apply(corners):
    mass_x = along_axis(MASS, corners, 1)
    stiff_x = along_axis(STIFF, corners, 1)
    mass_mass = along_axis(MASS, mass_x, 2)
    stiff_mass = along_axis(STIFF, mass_x, 2)
    mass_stiff = along_axis(MASS, stiff_x, 2)
    joined = [left + right for left, right in zip(stiff_mass, mass_stiff)]
    z_stiff = along_axis(STIFF, mass_mass, 4)
    z_mass = along_axis(MASS, joined, 4)
    return [left + right for left, right in zip(z_stiff, z_mass)]


def assemble_slab(parts):
    depth = parts[0].shape[0] - 1
    rows, cols = (parts[0].shape[1], parts[0].shape[2])
    total = jnp.zeros((depth, rows, cols), jnp.float32)
    for corner in range(8):
        a_z, b_y, c_x = (corner // 4, corner // 2 % 2, corner % 2)
        padded = jnp.pad(parts[corner], ((0, 0), (1, 0), (1, 0)))
        total = (
            total
            + padded[1 - a_z : 1 - a_z + depth, 1 - b_y : 1 - b_y + rows, 1 - c_x : 1 - c_x + cols]
        )
    return total


def corners_ext(extended, depth):
    rows, cols = (extended.shape[1], extended.shape[2])
    padded = jnp.pad(extended, ((0, 0), (0, 1), (0, 1)))
    return [
        padded[
            corner // 4 : corner // 4 + depth,
            corner // 2 % 2 : corner // 2 % 2 + rows,
            corner % 2 : corner % 2 + cols,
        ]
        for corner in range(8)
    ]


def coarse_cells(cells):
    depth, rows, cols = cells.shape
    blocks = cells.reshape(depth // 2, 2, rows // 2, 2, cols // 2, 2)
    return jnp.sum(blocks, axis=(1, 3, 5)) * 0.125


def restrict_axis(field, axis, below):
    length = field.shape[axis]
    even = lax.slice_in_dim(field, 0, length, 2, axis)
    odd = lax.slice_in_dim(field, 1, length, 2, axis)
    before = jnp.concatenate([below, lax.slice_in_dim(odd, 0, odd.shape[axis] - 1, 1, axis)], axis)
    return even + 0.5 * (odd + before)


def prolong_axis(coarse, axis, above):
    length = coarse.shape[axis]
    following = jnp.concatenate([lax.slice_in_dim(coarse, 1, length, 1, axis), above], axis)
    middle = 0.5 * (coarse + following)
    shape = list(coarse.shape)
    shape[axis] = 2 * length
    return jnp.stack([coarse, middle], axis + 1).reshape(shape)


def sweep(lam, resid, diagonal, operate, finish):
    theta = 0.5 * (UPPER + LOWER)
    delta = 0.5 * (UPPER - LOWER)
    ratio = theta / delta
    rho_now = 1.0 / ratio
    direction = resid / theta
    for step in range(DEG):
        lam = lam + direction
        if step < DEG - 1 or finish:
            resid = resid - operate(direction) / diagonal
        if step < DEG - 1:
            rho_next = 1.0 / (2.0 * ratio - rho_now)
            direction = rho_next * rho_now * direction + 2.0 * rho_next / delta * resid
            rho_now = rho_next
    return (lam, resid)


def solve(rhs, diagonal, coarse_diag, operate, from_below, from_above):
    lam = jnp.zeros_like(rhs)
    resid = rhs / diagonal
    lam, resid = sweep(lam, resid, diagonal, operate, True)
    fine = diagonal * resid
    coarse = restrict_axis(fine, 2, jnp.zeros_like(fine[:, :, :1]))
    coarse = restrict_axis(coarse, 1, jnp.zeros_like(coarse[:, :1, :]))
    coarse = restrict_axis(coarse, 0, from_below(coarse[-1:]))
    correction = OMEGA * coarse / coarse_diag
    refined = prolong_axis(correction, 0, from_above(correction[:1]))
    refined = prolong_axis(refined, 1, jnp.zeros_like(refined[:, :1, :]))
    refined = prolong_axis(refined, 2, jnp.zeros_like(refined[:, :, :1]))
    lam = lam + refined
    resid = resid - operate(refined) / diagonal
    lam, resid = sweep(lam, resid, diagonal, operate, False)
    return lam


def products(lam_corners, field_corners):
    applied = element_apply(field_corners)
    total = lam_corners[0] * applied[0]
    for corner in range(1, 8):
        total = total + lam_corners[corner] * applied[corner]
    return -total


def on_device(conductivity, forward_fields, receiver_pairs, observed):
    field = forward_fields[0]
    pairs = receiver_pairs[0]
    depth, rows, cols = conductivity.shape
    groups = observed.shape[0]
    receivers = observed.shape[1]
    group_index = lax.axis_index("src")
    cells_below = shifted(conductivity[depth - 2 :], "slab", 1)
    cond_ext = jnp.concatenate([cells_below[1:], conductivity], 0)
    diagonal = assemble_slab([cond_ext * (1.0 / 3.0) for corner in range(8)])
    coarse_ext = jnp.concatenate([coarse_cells(cells_below), coarse_cells(conductivity)], 0)
    coarse_diag = assemble_slab([coarse_ext * (2.0 / 3.0) for corner in range(8)])
    count = depth * rows * cols
    offsets = pairs - lax.axis_index("slab") * count
    inside = (offsets >= 0) & (offsets < count)
    safe = jnp.where(inside, offsets, 0)
    flat = field.reshape(-1)
    picked = jnp.where(inside, flat[safe], 0.0)
    partial_value = picked[:, 0] - picked[:, 1]
    predicted = lax.psum(partial_value, "slab")
    target = lax.dynamic_slice_in_dim(observed, group_index, 1, 0)[0]
    resid_data = predicted - target
    misfit_part = jnp.sum(0.5 * resid_data * resid_data)
    misfit = lax.psum(misfit_part, "src") / (groups * receivers)
    rhs = (
        jnp.zeros((count,), jnp.float32)
        .at[safe[:, 0]]
        .add(jnp.where(inside[:, 0], resid_data, 0.0))
    )
    rhs = (
        rhs.at[safe[:, 1]].add(jnp.where(inside[:, 1], -resid_data, 0.0)).reshape(depth, rows, cols)
    )

    def operate(vector):
        extended = with_halo(vector, (("slab", 0),), 1)
        corners = corners_ext(extended, depth + 1)
        return assemble_slab([cond_ext * part for part in element_apply(corners)])

    def from_below(plane):
        return shifted(plane, "slab", 1)

    def from_above(plane):
        return shifted(plane, "slab", -1)

    lam = solve(rhs, diagonal, coarse_diag, operate, from_below, from_above)
    lam_above, field_above = shifted((lam[:1], field[:1]), "slab", -1)
    lam_corners = corners_ext(jnp.concatenate([lam, lam_above], 0), depth)
    field_corners = corners_ext(jnp.concatenate([field, field_above], 0), depth)
    grad = products(lam_corners, field_corners)
    total = lax.psum(grad, "src")
    share = rows // groups
    gradient = lax.dynamic_slice_in_dim(total, group_index * share, share, 1)
    return (gradient, misfit)


def solution(mesh):
    in_specs = (P("slab", None, None), P("src", "slab", None, None), P("src", None, None), P())
    out_specs = (P("slab", "src", None), P())
    return jax.shard_map(
        on_device, mesh=mesh, in_specs=in_specs, out_specs=out_specs, check_vma=False
    )
```

profile of v0, /device:TPU:1, one launch (start us, length us, event | category | flops | bytes accessed | tf_op | source)
XLA Modules:
  0.0 576.2 jit_solution(2327984406747981708)
XLA Ops:
  7.2 1.4 slice.411
  8.6 4.6 collective-permute-start
  15.1 22.7 %gather_fusion = f32[4000]{0:T(1024)S(1)} fusion(f32[16384]{0:T(1024)S(1)} %bitcast.48, s32[4096]{0:T(1024)S(1)} %pad_clamp_fusion), kind=kCustom, calls=%fused_computation | custom fusion | bytes 48000 | tf_op jit(solution)/shard_map/gather | solution.py:171
  38.9 1.6 broadcast_select_fusion
  42.1 149.4 %psum.21 = f32[2000]{0:T(1024)S(1)} all-reduce(f32[2000]{0:T(1024)S(1)} %fusion.2), channel_id=1, replica_groups=mesh['src'=16,'slab'=32] {'slab'}, use_global_device_ids=true, to_apply=%region_0.1 | all-reduce | flops 2000 | bytes 16000 | tf_op jit(solution)/shard_map/psum | solution.py:173
  193.0 5.5 reshape.72
  198.6 2.5 reduce_sum.37
  201.1 14.3 %scatter_custom_fusion = f32[16384]{0:T(1024)S(1)} fusion(s32[2000]{0:T(1024)S(1)} %get-tuple-element.3, f32[2000]{0:T(1024)S(1)} %get-tuple-element.112, f32[]{:T(128)} %constant.20.clone.1), kind=kCustom, calls=%fused_computation.387 | custom fusion | flops 2000 | bytes 65540 | tf_op jit(solution)/shard_map/scatter-add | solution.py:181
  215.4 14.2 %scatter_fusion = f32[16384]{0:T(1024)S(1)} fusion(f32[16384]{0:T(1024)S(1)} %scatter_custom_fusion, s32[2000]{0:T(1024)S(1)} %get-tuple-element.2, f32[2000]{0:T(1024)S(1)} %get-tuple-element.111), kind=kCustom, calls=%fused_computation.2 | custom fusion | flops 2000 | bytes 32000 | tf_op jit(solution)/shard_map/scatter-add | solution.py:184
  231.9 1.3 collective-permute-start.2
  237.6 2.8 collective-permute-start.3
  240.4 1.5 collective-permute-start.4
  241.9 3.0 collective-permute-done.4
  248.6 1.9 collective-permute-start.5
  251.4 1.3 collective-permute-start.6
  252.7 3.4 collective-permute-done.6
  256.5 3.4 collective-permute-start.7
  260.0 1.3 collective-permute-start.8
  261.6 2.9 collective-permute-done.8
  267.0 4.0 collective-permute-start.9
  275.5 3.0 collective-permute-done.12
  279.7 66.8 %psum.23 = f32[]{:T(128)} all-reduce(f32[]{:T(128)} %get-tuple-element.110), channel_id=1, replica_groups=mesh['src'=16,'slab'=32] {'src'}, use_global_device_ids=true, to_apply=%region_8.9 | all-reduce | flops 1 | bytes 8 | tf_op jit(solution)/shard_map/psum | solution.py:177
  347.1 219.7 %all-reduce.38.cloned.1.call-done = f32[4,32,128]{2,1,0:T(8,128)} async-done(((f32[4,32,128]{2,1,0:T(8,128)}), f32[4,32,128]{2,1,0:T(8,128)}) %all-reduce.38.cloned.1.call-update) | async-done | bytes 65552 | tf_op jit(solution)/shard_map/psum | solution.py:203
  566.9 1.3 constant_dynamic-slice_fusion
  (112 shorter events, 25.8 us)
Async XLA Ops:
  7.2 184.3 %copy-start = (f32[16,2000]{1,0:T(8,128)S(1)}, f32[16,2000]{1,0:T(8,128)}, u32[]{:S(2)}) copy-start(f32[16,2000]{1,0:T(8,128)} %param.7) | copy-start | bytes 384004
  7.2 7.9 %copy-start.1 = (f32[1,4,32,128]{3,2,1,0:T(8,128)S(1)}, f32[1,4,32,128]{3,2,1,0:T(8,128)}, u32[]{:S(2)}) copy-start(f32[1,4,32,128]{3,2,1,0:T(8,128)} %param.5) | copy-start | bytes 196612
  7.2 559.7 %all-reduce.38.cloned.1.call-start = ((), (), s32[]{:S(2)}) async-start(), calls=%async_computation | async-start | bytes 131072 | tf_op jit(solution)/shard_map/psum | solution.py:203
  8.6 221.0 %collective-permute-start = (f32[2,32,128]{2,1,0:T(8,128)}, f32[2,32,128]{2,1,0:T(8,128)}, u32[]{:S(2)}, u32[]{:S(2)}) collective-permute-start(f32[2,32,128]{2,1,0:T(8,128)} %slice.411), channel_id=1, source_target_pairs={{0,1},{1,2},{2,3},{3,4},{4,5},{5,6},{6,7},{7,8},{8,9},{9,10},{10,1... | collective-permute-start | bytes 98312 | tf_op jit(solution)/shard_map/ppermute | solution.py:19
  14.3 23.5 %copy-start.3 = (s32[1,2000,2]{2,1,0:T(8,128)}, s32[1,2000,2]{2,1,0:T(8,128)S(1)}, u32[]{:S(2)}) copy-start(s32[1,2000,2]{2,1,0:T(8,128)S(1)} %copy.23) | copy-start | bytes 48004
  38.8 2.5 copy-start.4
  40.4 152.6 %copy-start.2 = (f32[4,32,128]{2,1,0:T(8,128)S(1)}, f32[4,32,128]{2,1,0:T(8,128)}, u32[]{:S(2)}) copy-start(f32[4,32,128]{2,1,0:T(8,128)} %param.4) | copy-start | bytes 196612
  230.6 4.6 collective-permute-start.1
  231.9 4.5 collective-permute-start.2
  237.6 4.3 collective-permute-start.3
  240.4 4.5 collective-permute-start.4
  248.6 2.7 collective-permute-start.5
  251.4 4.7 collective-permute-start.6
  256.5 5.1 collective-permute-start.7
  260.0 4.5 collective-permute-start.8
  265.7 6.6 %collective-permute-start.10 = (f32[1,32,128]{2,1,0:T(8,128)S(1)}, f32[1,32,128]{2,1,0:T(8,128)S(1)}, u32[]{:S(2)}, u32[]{:S(2)}) collective-permute-start(f32[1,32,128]{2,1,0:T(8,128)S(1)} %get-tuple-element.105), channel_id=1, source_target_pairs={{1,0},{2,1},{3,2},{4,3},{5,4},{6,5},{7,6},{8,7},{9,8},{10,9},{11,1... | collective-permute-start | bytes 49160 | tf_op jit(solution)/shard_map/ppermute | solution.py:30
  267.0 5.3 collective-permute-start.9
  271.0 4.5 collective-permute-start.11
  273.5 5.1 collective-permute-start.12
Sparse Core Ops, SparseCore 0:
  279.8 287.0 all-reduce.37
where the time goes:
time: 577 us; the launch traced here: 576 us
  waiting for transfers between devices  235 us (41%)
  blocking collectives  216 us (37%)
  other arithmetic  42.3 us (7%)
  local copies, waits for them, and re-layouts  39.2 us (7%)
  starting transfers between devices  27.3 us (5%)
  between operations  16.5 us (3%)
    psum x1, waiting for transfers between devices, on_device(): total = lax.psum(grad, 'src')  220 us
    psum x1, blocking collectives, on_device(): predicted = lax.psum(partial_value, 'slab')  149 us
    psum x1, blocking collectives, on_device(): misfit = lax.psum(misfit_part, 'src') / (groups * receivers)  66.8 us
    gather x2, local copies, waits for them, and re-layouts, on_device(): picked = jnp.where(inside, flat[safe], 0.0)  23.7 us
    scatter-add x1, other arithmetic, on_device(): rhs = jnp.zeros((count,), jnp.float32).at[safe[:, 0]].add(jnp.where(insid...  14.3 us
    scatter-add x1, other arithmetic, on_device(): rhs.at[safe[:, 1]].add(jnp.where(inside[:, 1], -resid_data, 0.0))  14.2 us
  transfers between devices with their start and end apart: 14, of which 8 were waited for; matrix products, arithmetic and copies ran while one was open for 12% of the time, Pallas kernels for 0%

commit v1 on v0

v1 whole, which is shorter than its diff:
```python
import functools

import jax
import jax.numpy as jnp
from jax import lax
from jax.experimental import pallas as pl
from jax.experimental.pallas import tpu as pltpu
from jax.sharding import PartitionSpec as P

LOWER = 0.3
UPPER = 2.0
OMEGA = 0.6
THETA = 0.5 * (UPPER + LOWER)
DELTA = 0.5 * (UPPER - LOWER)
RATIO = THETA / DELTA
RHO_A = 1.0 / RATIO
RHO_B = 1.0 / (2.0 * RATIO - RHO_A)
ALPHA = RHO_B * RHO_A
BETA = 2.0 * RHO_B / DELTA

NY, NX = 32, 128
DEPTH = 4
BELOW = 5
PLANES = 15
CELLS = 16
RX = 2000
RROWS = 16
IDX = 2 * RROWS
GROUPS = 16
NZ = 128
MESH = pl.DeviceIdType.MESH
F32 = jnp.float32
ONE, TWO, THREE = 1.0 / 16.0, 1.0 / 24.0, 1.0 / 48.0


def lanes():
    return lax.broadcasted_iota(jnp.int32, (NY, NX), 1)


def rows():
    return lax.broadcasted_iota(jnp.int32, (NY, NX), 0)


def next_x(v):
    return jnp.where(lanes() < NX - 1, pltpu.roll(v, NX - 1, 1), 0.0)


def prev_x(v):
    return jnp.where(lanes() > 0, pltpu.roll(v, 1, 1), 0.0)


def next_y(v):
    return jnp.where(rows() < NY - 1, pltpu.roll(v, NY - 1, 0), 0.0)


def prev_y(v):
    return jnp.where(rows() > 0, pltpu.roll(v, 1, 0), 0.0)


def prev2_x(v):
    return jnp.where(lanes() > 1, pltpu.roll(v, 2, 1), 0.0)


def prev2_y(v):
    return jnp.where(rows() > 1, pltpu.roll(v, 2, 0), 0.0)


def forward(v):
    moved = next_x(v)
    sx, dx = v + moved, v - moved
    ms, md = next_y(sx), next_y(dx)
    return sx + ms, sx - ms, dx + md, dx - md


def cell_terms(low, high):
    ss, ds, sd, dd = low
    ss2, ds2, sd2, dd2 = high
    return (ss - ss2, ds + ds2, ds - ds2, sd + sd2, sd - sd2, dd + dd2, dd - dd2)


def scatter_cell(low, high, c1, c2, c3):
    zss, sds, zds, ssd, zsd, sdd, zdd = cell_terms(low, high)
    zss = zss * c1
    sds, zds = sds * c1, zds * c2
    ssd, zsd = ssd * c1, zsd * c2
    sdd, zdd = sdd * c2, zdd * c3
    lower = (zss, sds + zds, ssd + zsd, sdd + zdd)
    upper = (-zss, sds - zds, ssd - zsd, sdd - zdd)
    return lower, upper


def backward(parts):
    ss, ds, sd, dd = parts
    os = (ss + ds) + prev_y(ss - ds)
    od = (sd + dd) + prev_y(sd - dd)
    return (os + od) + prev_x(os - od)


def apply_planes(v_ref, coef, first, last, sink):
    low = forward(v_ref[first - 1])
    mid = forward(v_ref[first])
    _, upper = scatter_cell(low, mid, coef[0, first - 1], coef[1, first - 1], coef[2, first - 1])

    def body(p, carry):
        here, above = carry[:4], carry[4:]
        ahead = forward(v_ref[p + 1])
        lower, upper = scatter_cell(here, ahead, coef[0, p], coef[1, p], coef[2, p])
        sink(p, backward([a + b for a, b in zip(lower, above)]))
        return (*ahead, *upper)

    lax.fori_loop(first, last + 1, body, (*mid, *upper))


def kernel(
    cond_hbm, field_hbm, pairs_hbm, obs_hbm,
    grad_ref, misfit_ref,
    cext, fext, pairs, obs, index, target,
    part, recv_xy, zsum, recv_z,
    row_at, lane_at, res_at, row_hot, lane_res, coef, diag, invd, cinv, hu,
    resid, direct, work, lam, pe, fine,
    mis, recv_mis, chunks, recv_core, merged, recv_src,
    in_sem, send_sem, halo_sem, xy_sem, z_sem, mis_sem, core_sem, src_sem,
):
    src = lax.axis_index("src")
    slab = lax.axis_index("slab")
    zl, core = src // 2, src % 2
    zh, px, py = slab // 16, (slab // 4) % 4, slab % 4
    plane_peers = [
        (src, zh * 16 + ((px + i) % 4) * 4 + (py + j) % 4)
        for i in range(4)
        for j in range(4)
        if i + j
    ]
    z_peer = (src, (1 - zh) * 16 + px * 4 + py)
    ups = [(src, (slab + k) % 32) for k in (1, 2)]
    downs = [(src, (slab + 32 - k) % 32) for k in (1, 2)]
    src_peers = [(((zl + i) % 8) * 2 + (core + j) % 2, slab) for i in range(8) for j in range(2) if i + j]
    sibling = (zl * 2 + 1 - core, slab)
    run_peers = [(zl + i) % 8 for i in range(1, 8)]

    barrier = pltpu.get_barrier_semaphore()
    greeted = plane_peers + [z_peer] + ups + downs + src_peers
    for peer in greeted:
        pl.semaphore_signal(barrier, inc=1, device_id=peer, device_id_type=MESH)

    loads = [
        pltpu.make_async_copy(field_hbm, fext.at[pl.ds(0, DEPTH)], in_sem.at[0]),
        pltpu.make_async_copy(pairs_hbm, pairs, in_sem.at[1]),
        pltpu.make_async_copy(cond_hbm, cext.at[pl.ds(6, DEPTH)], in_sem.at[2]),
        pltpu.make_async_copy(obs_hbm, obs, in_sem.at[3]),
    ]
    for load in loads:
        load.start()
    for load in loads:
        load.wait()

    index[...] = jnp.full((IDX, NX), 1 << 24, jnp.int32)
    target[...] = jnp.zeros((RROWS, NX), F32)
    for j in range(RROWS):
        width = min(NX, RX - j * NX)
        span = pl.ds(j * NX, width)
        for at, end in ((j, 0), (RROWS + j, 1)):
            index[at : at + 1, 0:width] = pairs[end : end + 1, span]
        mine = lax.broadcasted_iota(jnp.int32, (GROUPS, width), 0) == src
        target[j : j + 1, 0:width] = jnp.sum(
            jnp.where(mine, obs[:, span], 0.0), axis=0, keepdims=True
        )

    lane = jnp.bitwise_and(index[...], NX - 1)
    line = jnp.right_shift(index[...], 7) - slab * (DEPTH * NY)

    def pick(block, acc):
        values = fext[block // 4, pl.ds((block % 4) * 8, 8), :]
        for k in range(8):
            spread = jnp.broadcast_to(values[k : k + 1, :], (IDX, NX))
            found = jnp.take_along_axis(spread, lane, axis=1, mode="promise_in_bounds")
            acc = jnp.where(line == block * 8 + k, found, acc)
        return acc

    picked = lax.fori_loop(0, DEPTH * NY // 8, pick, jnp.zeros((IDX, NX), F32))
    part[...] = picked[:RROWS] - picked[RROWS:]
    here = px * 4 + py
    recv_xy[here] = part[...]

    pl.semaphore_wait(barrier, len(greeted))

    def remote(source, dest, arrival, peer):
        return pltpu.make_async_remote_copy(
            src_ref=source, dst_ref=dest, send_sem=send_sem, recv_sem=arrival,
            device_id=peer, device_id_type=MESH,
        )

    sent = []

    def send(source, dest, arrival, peer):
        copy = remote(source, dest, arrival, peer)
        copy.start()
        sent.append(copy)

    def arrived(buffer, arrival):
        pltpu.make_async_copy(buffer, buffer, arrival).wait()

    for peer in plane_peers:
        send(part, recv_xy.at[here], xy_sem, peer)
    own = cext.at[pl.ds(6, DEPTH)]
    send(own, cext.at[pl.ds(2, DEPTH)], halo_sem.at[0], ups[0])
    send(own, cext.at[pl.ds(10, DEPTH)], halo_sem.at[1], downs[0])
    send(cext.at[pl.ds(8, 2)], cext.at[pl.ds(0, 2)], halo_sem.at[2], ups[1])
    send(cext.at[pl.ds(6, 2)], cext.at[pl.ds(14, 2)], halo_sem.at[3], downs[1])
    send(fext.at[pl.ds(0, 1)], fext.at[pl.ds(DEPTH, 1)], halo_sem.at[4], downs[0])

    place = jnp.right_shift(index[...], 7) - (slab * DEPTH - BELOW) * NY
    for j in range(IDX):
        row_at[j] = place[j : j + 1, :].astype(F32)
        lane_at[j] = lane[j : j + 1, :].astype(F32)

    def hot(j, carry):
        spread = jnp.broadcast_to(row_at[j], (PLANES * NY, NX))
        line_id = lax.broadcasted_iota(jnp.int32, (PLANES * NY, NX), 0).astype(F32)
        row_hot[j] = jnp.where(spread == line_id, 1.0, 0.0).astype(jnp.bfloat16)
        return carry

    lax.fori_loop(0, IDX, hot, 0)

    arrived(recv_xy.at[pl.ds(0, 15)], xy_sem)

    def add_xy(k, acc):
        return acc + recv_xy[k]

    zsum[...] = lax.fori_loop(1, 16, add_xy, recv_xy[0])
    send(zsum, recv_z, z_sem, z_peer)

    arrived(cext.at[pl.ds(2, DEPTH)], halo_sem.at[0])
    arrived(cext.at[pl.ds(10, DEPTH)], halo_sem.at[1])
    arrived(cext.at[pl.ds(0, 2)], halo_sem.at[2])
    arrived(cext.at[pl.ds(14, 2)], halo_sem.at[3])
    arrived(fext.at[pl.ds(DEPTH, 1)], halo_sem.at[4])

    def inside(plane):
        z = slab * DEPTH + plane
        return jnp.logical_and(z >= 0, z < NZ)

    def masked_cells(e):
        return jnp.where(inside(e - 6), cext[e], 0.0)

    def around(cells):
        along = cells + prev_x(cells)
        return along + prev_y(along)

    def diagonals(p, below):
        cells = masked_cells(p + 1)
        coef[0, p] = cells * ONE
        coef[1, p] = cells * TWO
        coef[2, p] = cells * THREE
        boxed = around(cells)
        value = (boxed + below) * (1.0 / 3.0)
        keep = inside(p - BELOW)
        diag[p] = jnp.where(keep, value, 0.0)
        invd[p] = jnp.where(keep, 1.0 / jnp.where(keep, value, 1.0), 0.0)
        return boxed

    lax.fori_loop(0, PLANES, diagonals, around(masked_cells(0)))

    even = jnp.logical_and(lanes() % 2 == 0, rows() % 2 == 0)

    def coarse_box(j):
        pair = masked_cells(2 * j + 2) + masked_cells(2 * j + 3)
        pair = pair + next_y(pair)
        pair = jnp.where(even, pair + next_x(pair), 0.0)
        pair = pair + prev2_x(pair)
        return pair + prev2_y(pair)

    def coarse(j, below):
        boxed = coarse_box(j)
        value = (boxed + below) * (0.125 * 2.0 / 3.0)
        keep = jnp.logical_and(even, inside(2 * (j - 2)))
        cinv[j - 1] = jnp.where(keep, OMEGA / jnp.where(keep, value, 1.0), 0.0)
        return boxed

    lax.fori_loop(1, 6, coarse, coarse_box(0))

    def field_terms(p, low):
        plane = jnp.where(inside(p + 1), fext[p + 1], 0.0)
        high = forward(plane)
        scales = (-ONE, -ONE, -TWO, -ONE, -TWO, -TWO, -THREE)
        for k, (term, scale) in enumerate(zip(cell_terms(low, high), scales)):
            hu[p, k] = term * scale
        return high

    lax.fori_loop(0, DEPTH, field_terms, forward(fext[0]))

    arrived(recv_z, z_sem)
    res = (zsum[...] + recv_z[...]) - target[...]
    half = jnp.sum(jnp.sum(0.5 * res * res, axis=0, keepdims=True), axis=1, keepdims=True)
    mis[...] = jnp.broadcast_to(half, (1, NX))
    recv_mis[src] = mis[...]
    for peer in src_peers:
        send(mis, recv_mis.at[src], mis_sem, peer)

    for j in range(RROWS):
        res_at[j] = res[j : j + 1, :]
        res_at[RROWS + j] = -res[j : j + 1, :]

    def spread_res(j, carry):
        value = jnp.broadcast_to(res_at[j], (NX, NX))
        at = jnp.broadcast_to(lane_at[j], (NX, NX))
        lane_id = lax.broadcasted_iota(jnp.int32, (NX, NX), 0).astype(F32)
        value = jnp.where(at == lane_id, value, 0.0)
        high = value.astype(jnp.bfloat16)
        lane_res[j, 0:NX, :] = high
        lane_res[j, NX:, :] = (value - high.astype(F32)).astype(jnp.bfloat16)
        return carry

    lax.fori_loop(0, IDX, spread_res, 0)

    def product(j, acc):
        both = lax.dot_general(
            row_hot[j], lane_res[j], (((1,), (1,)), ((), ())), preferred_element_type=F32
        )
        fine[...] += both
        return acc

    fine[...] = jnp.zeros_like(fine)
    lax.fori_loop(0, IDX, product, 0)

    def start_resid(p, carry):
        block = fine[pl.ds(pl.multiple_of(p * NY, NY), NY), :]
        resid[p] = (block[:, :NX] + block[:, NX:]) * invd[p]
        return carry

    lax.fori_loop(0, PLANES, start_resid, 0)

    def first_step(p, applied):
        r = resid[p]
        r1 = r - (applied * (1.0 / THETA)) * invd[p]
        d2 = (ALPHA / THETA) * r + BETA * r1
        resid[p] = r1
        direct[p] = d2
        lam[p] = r * (1.0 / THETA) + d2

    apply_planes(resid, coef, 1, 13, first_step)

    def second_step(p, applied):
        r2 = resid[p] - applied * invd[p]
        resid[p] = r2
        f = diag[p] * r2
        f = f + 0.5 * (prev_x(f) + next_x(f))
        work[p] = f + 0.5 * (prev_y(f) + next_y(f))

    apply_planes(direct, coef, 2, 12, second_step)

    def correct(j):
        p = 2 * j + 3
        c = (work[p] + 0.5 * (work[p - 1] + work[p + 1])) * cinv[j]
        c = c + 0.5 * (prev_y(c) + next_y(c))
        return c + 0.5 * (prev_x(c) + next_x(c))

    def prolong(j, below):
        c = correct(j)
        pe[2 * j + 3] = c
        pe[2 * j + 2] = 0.5 * (below + c)
        return c

    first = correct(0)
    pe[3] = first
    lax.fori_loop(1, 5, prolong, first)

    def third_step(p, applied):
        r3 = resid[p] - applied * invd[p]
        resid[p] = r3
        lam[p] = lam[p] + pe[p] + r3 * (1.0 / THETA)

    apply_planes(pe, coef, 4, 10, third_step)

    def fourth_step(p, applied):
        r3 = resid[p]
        r4 = r3 - (applied * (1.0 / THETA)) * invd[p]
        lam[p] = lam[p] + (ALPHA / THETA) * r3 + BETA * r4

    apply_planes(resid, coef, 5, 9, fourth_step)

    low = forward(lam[BELOW])
    for p in range(DEPTH):
        high = forward(lam[BELOW + p + 1])
        total = None
        for k, term in enumerate(cell_terms(low, high)):
            piece = term * hu[p, k]
            total = piece if total is None else total + piece
        low = high
        for z in range(8):
            for c in range(2):
                at = 4 * z + 2 * c
                chunks[c, z, 2 * p : 2 * p + 2, :] = total[at : at + 2, :]

    send(chunks.at[1 - core], recv_core, core_sem, sibling)
    arrived(recv_core, core_sem)
    merged[...] = chunks[core] + recv_core[...]
    for z in run_peers:
        send(merged.at[z], recv_src.at[zl], src_sem, (z * 2 + core, slab))
    recv_src[zl] = merged[zl]
    arrived(recv_mis.at[pl.ds(0, 15)], mis_sem)
    misfit = recv_mis[0]
    for k in range(1, GROUPS):
        misfit = misfit + recv_mis[k]
    misfit_ref[...] = misfit * (1.0 / (GROUPS * RX))
    arrived(recv_src.at[pl.ds(0, 7)], src_sem)
    total = recv_src[0]
    for k in range(1, 8):
        total = total + recv_src[k]
    grad_ref[...] = total
    for copy in sent:
        copy.wait_send()


def on_device(conductivity, forward_fields, receiver_pairs, observed):
    field = forward_fields.reshape(DEPTH, NY, NX)
    pairs = jnp.transpose(receiver_pairs[0])
    plane = (NY, NX)
    any_spec = pl.BlockSpec(memory_space=pl.ANY)
    vmem = pl.BlockSpec(memory_space=pltpu.VMEM)
    dma = pltpu.SemaphoreType.DMA
    grad, misfit = pl.pallas_call(
        kernel,
        name="adjoint_gradient",
        out_shape=(jax.ShapeDtypeStruct((8, NX), F32), jax.ShapeDtypeStruct((1, NX), F32)),
        in_specs=[any_spec] * 4,
        out_specs=(vmem, vmem),
        scratch_shapes=[
            pltpu.VMEM((CELLS, *plane), F32),
            pltpu.VMEM((DEPTH + 1, *plane), F32),
            pltpu.VMEM((2, RX), jnp.int32),
            pltpu.VMEM((GROUPS, RX), F32),
            pltpu.VMEM((IDX, NX), jnp.int32),
            pltpu.VMEM((RROWS, NX), F32),
            pltpu.VMEM((RROWS, NX), F32),
            pltpu.VMEM((16, RROWS, NX), F32),
            pltpu.VMEM((RROWS, NX), F32),
            pltpu.VMEM((RROWS, NX), F32),
            pltpu.VMEM((IDX, 1, NX), F32),
            pltpu.VMEM((IDX, 1, NX), F32),
            pltpu.VMEM((IDX, 1, NX), F32),
            pltpu.VMEM((IDX, PLANES * NY, NX), jnp.bfloat16),
            pltpu.VMEM((IDX, 2 * NX, NX), jnp.bfloat16),
            pltpu.VMEM((3, PLANES, *plane), F32),
            pltpu.VMEM((PLANES, *plane), F32),
            pltpu.VMEM((PLANES, *plane), F32),
            pltpu.VMEM((5, *plane), F32),
            pltpu.VMEM((DEPTH, 7, *plane), F32),
            pltpu.VMEM((PLANES, *plane), F32),
            pltpu.VMEM((PLANES, *plane), F32),
            pltpu.VMEM((PLANES, *plane), F32),
            pltpu.VMEM((PLANES, *plane), F32),
            pltpu.VMEM((PLANES, *plane), F32),
            pltpu.VMEM((PLANES * NY, 2 * NX), F32),
            pltpu.VMEM((1, NX), F32),
            pltpu.VMEM((GROUPS, 1, NX), F32),
            pltpu.VMEM((2, 8, 8, NX), F32),
            pltpu.VMEM((8, 8, NX), F32),
            pltpu.VMEM((8, 8, NX), F32),
            pltpu.VMEM((8, 8, NX), F32),
            dma((4,)), dma, dma((5,)), dma, dma, dma, dma, dma,
        ],
        compiler_params=pltpu.CompilerParams(
            collective_id=0, has_side_effects=True, vmem_limit_bytes=32 * 1024 * 1024
        ),
    )(conductivity, field, pairs, observed)
    return grad.reshape(DEPTH, 2, NX), misfit[0, 0]


def solution(mesh):
    in_specs = (P("slab", None, None), P("src", "slab", None, None), P("src", None, None), P())
    out_specs = (P("slab", "src", None), P())
    return jax.shard_map(
        on_device, mesh=mesh, in_specs=in_specs, out_specs=out_specs, check_vma=False
    )
```

time: 577 us -> 64.1 us (0.11)
  waiting for transfers between devices: 235 us -> 0 us
  blocking collectives: 216 us -> 0 us
  Pallas kernels: 0 us -> 58.1 us
  other arithmetic: 42.3 us -> 0 us
  local copies, waits for them, and re-layouts: 39.2 us -> 3.89 us
  starting transfers between devices: 27.3 us -> 0 us
  between operations: 16.5 us -> 1.82 us
    psum x1 -> x0, waiting for transfers between devices: 220 us -> none  [on_device(): total = lax.psum(grad, 'src')]
    psum x2 -> x0, blocking collectives: 216 us -> none  [the longest x1 149 us: on_device(): predicted = lax.psum(partial_value, 'slab')]
    pallas_call x0 -> x1, Pallas kernels: none -> 58.1 us  [on_device(): pl.pallas_call(kernel, name='adjoint_gradient', out_shape=(jax.ShapeDtype...]
    scatter-add x2 -> x0, other arithmetic: 28.5 us -> none  [the longest x1 14.3 us: on_device(): rhs = jnp.zeros((count,), jnp.float32).at[safe[:, 0]].add(jnp.where(insid...]
    ppermute x13 -> x0, starting transfers between devices: 27.3 us -> none  [the longest x4 11.5 us: with_halo(): lax.ppermute(lax.slice_in_dim(block, block.shape[dim] - width, None, axis...]
    gather x2 -> x0, local copies, waits for them, and re-layouts: 23.7 us -> none  [on_device(): picked = jnp.where(inside, flat[safe], 0.0)]
    ppermute x13 -> x0, waiting for transfers between devices: 14.9 us -> none  [the longest x5 7.9 us: shifted(): return lax.ppermute(array, axis, pairs)]
  transfers between devices with their start and end apart: 14 -> 0, of which waited for: 8 -> 0; matrix products, arithmetic and copies ran while one was open for 12% -> 0% of each run, Pallas kernels for 0% -> 0%
where the time goes in v1:
time: 64.1 us; the launch traced here: 63.8 us
  Pallas kernels  58.1 us (91%)
  local copies, waits for them, and re-layouts  3.89 us (6%)
  between operations  1.82 us (3%)
    pallas_call x1, Pallas kernels, on_device(): pl.pallas_call(kernel, name='adjoint_gradient', out_shape=(jax.ShapeDtype...  58.1 us
    unnamed x9, local copies, waits for them, and re-layouts  3.89 us

profile of v1, /device:TPU:1, one launch (start us, length us, event | category | flops | bytes accessed | tf_op | source)
XLA Modules:
  0.0 63.8 jit_solution(15646775020705142671)
XLA Ops:
  0.6 0.0 copy-start
  0.6 0.9 %copy-done = f32[16,2000]{1,0:T(8,128)S(1)} copy-done((f32[16,2000]{1,0:T(8,128)S(1)}, f32[16,2000]{1,0:T(8,128)}, u32[]{:S(2)}) %copy-start) | copy-done | bytes 128024
  1.5 0.0 copy-start.1
  1.5 0.8 %copy-done.1 = f32[4,32,128]{2,1,0:T(8,128)S(1)} copy-done((f32[4,32,128]{2,1,0:T(8,128)S(1)}, f32[4,32,128]{2,1,0:T(8,128)}, u32[]{:S(2)}) %copy-start.1) | copy-done | bytes 65560
  2.4 0.0 copy-start.2
  2.4 0.8 %copy-done.2 = f32[1,4,32,128]{3,2,1,0:T(8,128)S(1)} copy-done((f32[1,4,32,128]{3,2,1,0:T(8,128)S(1)}, f32[1,4,32,128]{3,2,1,0:T(8,128)}, u32[]{:S(2)}) %copy-start.2) | copy-done | bytes 65560
  3.2 0.0 copy-start.3
  3.2 0.7 %copy-done.3 = s32[1,2000,2]{1,2,0:T(2,128)S(1)} copy-done((s32[1,2000,2]{1,2,0:T(2,128)S(1)}, s32[1,2000,2]{1,2,0:T(2,128)}, u32[]{:S(2)}) %copy-start.3) | copy-done | bytes 16024
  3.9 58.1 %adjoint_gradient.1 = (f32[8,128]{1,0:T(8,128)S(1)}, f32[1,128]{1,0:T(1,128)S(1)}) custom-call(f32[4,32,128]{2,1,0:T(8,128)S(1)} %copy-done.1, f32[4,32,128]{2,1,0:T(8,128)S(1)} %bitcast.7, s32[2,2000]{1,0:T(2,128)S(1)} %bitcast.8, f32[16,2000]{1,0:T(8,128)S(1)} %copy-done), custom_call_target="tpu_custom_call" | custom-call | tf_op jit(solution)/shard_map/adjoint_gradient/pallas_call | solution.py:422
  62.0 0.6 copy.8
Async XLA Ops:
  0.6 0.9 %copy-start = (f32[16,2000]{1,0:T(8,128)S(1)}, f32[16,2000]{1,0:T(8,128)}, u32[]{:S(2)}) copy-start(f32[16,2000]{1,0:T(8,128)} %obs_hbm.1) | copy-start | bytes 384004
  1.5 0.8 %copy-start.1 = (f32[4,32,128]{2,1,0:T(8,128)S(1)}, f32[4,32,128]{2,1,0:T(8,128)}, u32[]{:S(2)}) copy-start(f32[4,32,128]{2,1,0:T(8,128)} %cond_hbm.1) | copy-start | bytes 196612
  2.4 0.8 %copy-start.2 = (f32[1,4,32,128]{3,2,1,0:T(8,128)S(1)}, f32[1,4,32,128]{3,2,1,0:T(8,128)}, u32[]{:S(2)}) copy-start(f32[1,4,32,128]{3,2,1,0:T(8,128)} %param.5) | copy-start | bytes 196612
  3.2 0.7 %copy-start.3 = (s32[1,2000,2]{1,2,0:T(2,128)S(1)}, s32[1,2000,2]{1,2,0:T(2,128)}, u32[]{:S(2)}) copy-start(s32[1,2000,2]{1,2,0:T(2,128)} %param.6) | copy-start | bytes 48004

commit v2 on v1

v2 whole, which is shorter than its diff:
```python
import functools

import jax
import jax.numpy as jnp
from jax import lax
from jax.experimental import pallas as pl
from jax.experimental.pallas import tpu as pltpu
from jax.sharding import PartitionSpec as P

LOWER = 0.3
UPPER = 2.0
OMEGA = 0.6
THETA = 0.5 * (UPPER + LOWER)
DELTA = 0.5 * (UPPER - LOWER)
RATIO = THETA / DELTA
RHO_A = 1.0 / RATIO
RHO_B = 1.0 / (2.0 * RATIO - RHO_A)
ALPHA = RHO_B * RHO_A
BETA = 2.0 * RHO_B / DELTA

NY, NX = 32, 128
DEPTH = 4
BELOW = 5
BLOCK = 15
PLANES = 15
CELLS = 16
RX = 2000
RROWS = 16
IDX = 2 * RROWS
GROUPS = 16
NZ = 128
MESH = pl.DeviceIdType.MESH
F32 = jnp.float32
ONE, TWO, THREE = 1.0 / 16.0, 1.0 / 24.0, 1.0 / 48.0


def lanes():
    return lax.broadcasted_iota(jnp.int32, (NY, NX), 1)


def rows():
    return lax.broadcasted_iota(jnp.int32, (NY, NX), 0)


def next_x(v):
    return jnp.where(lanes() < NX - 1, pltpu.roll(v, NX - 1, 1), 0.0)


def prev_x(v):
    return jnp.where(lanes() > 0, pltpu.roll(v, 1, 1), 0.0)


def next_y(v):
    return jnp.where(rows() < NY - 1, pltpu.roll(v, NY - 1, 0), 0.0)


def prev_y(v):
    return jnp.where(rows() > 0, pltpu.roll(v, 1, 0), 0.0)


def prev2_x(v):
    return jnp.where(lanes() > 1, pltpu.roll(v, 2, 1), 0.0)


def prev2_y(v):
    return jnp.where(rows() > 1, pltpu.roll(v, 2, 0), 0.0)


def forward(v):
    moved = next_x(v)
    sx, dx = v + moved, v - moved
    ms, md = next_y(sx), next_y(dx)
    return sx + ms, sx - ms, dx + md, dx - md


def cell_terms(low, high):
    ss, ds, sd, dd = low
    ss2, ds2, sd2, dd2 = high
    return (ss - ss2, ds + ds2, ds - ds2, sd + sd2, sd - sd2, dd + dd2, dd - dd2)


def scatter_cell(low, high, c1, c2, c3):
    zss, sds, zds, ssd, zsd, sdd, zdd = cell_terms(low, high)
    zss = zss * c1
    sds, zds = sds * c1, zds * c2
    ssd, zsd = ssd * c1, zsd * c2
    sdd, zdd = sdd * c2, zdd * c3
    lower = (zss, sds + zds, ssd + zsd, sdd + zdd)
    upper = (-zss, sds - zds, ssd - zsd, sdd - zdd)
    return lower, upper


def backward(parts):
    ss, ds, sd, dd = parts
    os = (ss + ds) + prev_y(ss - ds)
    od = (sd + dd) + prev_y(sd - dd)
    return (os + od) + prev_x(os - od)


def apply_planes(v_ref, coef, first, last, sink):
    low = forward(v_ref[first - 1])
    mid = forward(v_ref[first])
    _, upper = scatter_cell(low, mid, coef[0, first - 1], coef[1, first - 1], coef[2, first - 1])

    def body(p, carry):
        here, above = carry[:4], carry[4:]
        ahead = forward(v_ref[p + 1])
        lower, upper = scatter_cell(here, ahead, coef[0, p], coef[1, p], coef[2, p])
        sink(p, backward([a + b for a, b in zip(lower, above)]))
        return (*ahead, *upper)

    lax.fori_loop(first, last + 1, body, (*mid, *upper), unroll=True)


def read_pairs(pairs, index, place_row, lane_row, slab):
    index[...] = jnp.full((IDX, NX), 1 << 24, jnp.int32)
    for j in range(RROWS):
        width = min(NX, RX - j * NX)
        for at, end in ((j, 0), (RROWS + j, 1)):
            index[at : at + 1, 0:width] = pairs[end : end + 1, pl.ds(j * NX, width)]
    lane = jnp.bitwise_and(index[...], NX - 1).astype(F32)
    place = (jnp.right_shift(index[...], 7) - (slab * DEPTH - BELOW) * NY).astype(F32)
    for j in range(IDX):
        place_row[j] = place[j : j + 1, :]
        lane_row[j] = lane[j : j + 1, :]


def read_target(obs, target, src):
    target[...] = jnp.zeros((RROWS, NX), F32)
    for j in range(RROWS):
        width = min(NX, RX - j * NX)
        mine = lax.broadcasted_iota(jnp.int32, (GROUPS, width), 0) == src
        target[j : j + 1, 0:width] = jnp.sum(
            jnp.where(mine, obs[:, pl.ds(j * NX, width)], 0.0), axis=0, keepdims=True
        )


def gather(fext, index, part, slab):
    lane = jnp.bitwise_and(index[...], NX - 1)
    line = jnp.right_shift(index[...], 7) - slab * (DEPTH * NY)

    def pick(block, acc):
        values = fext[block // 4, pl.ds((block % 4) * 8, 8), :]
        for k in range(8):
            spread = jnp.broadcast_to(values[k : k + 1, :], (IDX, NX))
            found = jnp.take_along_axis(spread, lane, axis=1, mode="promise_in_bounds")
            acc = jnp.where(line == block * 8 + k, found, acc)
        return acc

    picked = lax.fori_loop(0, DEPTH * NY // 8, pick, jnp.zeros((IDX, NX), F32))
    part[...] = picked[:RROWS] - picked[RROWS:]


def one_hot_rows(place_row, row_hot):
    def hot(j, carry):
        spread = jnp.broadcast_to(place_row[j], (PLANES * NY, NX))
        line_id = lax.broadcasted_iota(jnp.int32, (PLANES * NY, NX), 0).astype(F32)
        row_hot[:, pl.ds(pl.multiple_of(j * NX, NX), NX)] = jnp.where(spread == line_id, 1.0, 0.0).astype(jnp.bfloat16)
        return carry

    lax.fori_loop(0, IDX, hot, 0)


def inside(plane, slab):
    z = slab * DEPTH + plane
    return jnp.logical_and(z >= 0, z < NZ)


def conductivity_terms(cext, coef, diag, invd, cinv, slab):
    def masked_cells(e):
        return jnp.where(inside(e - 6, slab), cext[e], 0.0)

    def around(cells):
        along = cells + prev_x(cells)
        return along + prev_y(along)

    def diagonals(p, below):
        cells = masked_cells(p + 1)
        coef[0, p] = cells * ONE
        coef[1, p] = cells * TWO
        coef[2, p] = cells * THREE
        boxed = around(cells)
        value = (boxed + below) * (1.0 / 3.0)
        keep = inside(p - BELOW, slab)
        diag[p] = jnp.where(keep, value, 0.0)
        invd[p] = jnp.where(keep, 1.0 / jnp.where(keep, value, 1.0), 0.0)
        return boxed

    lax.fori_loop(0, PLANES, diagonals, around(masked_cells(0)))

    even = jnp.logical_and(lanes() % 2 == 0, rows() % 2 == 0)

    def coarse_box(j):
        pair = masked_cells(2 * j + 2) + masked_cells(2 * j + 3)
        pair = pair + next_y(pair)
        pair = jnp.where(even, pair + next_x(pair), 0.0)
        pair = pair + prev2_x(pair)
        return pair + prev2_y(pair)

    def coarse(j, below):
        boxed = coarse_box(j)
        value = (boxed + below) * (0.125 * 2.0 / 3.0)
        keep = jnp.logical_and(even, inside(2 * (j - 2), slab))
        cinv[j - 1] = jnp.where(keep, OMEGA / jnp.where(keep, value, 1.0), 0.0)
        return boxed

    lax.fori_loop(1, 6, coarse, coarse_box(0))


def field_terms(fext, hu, slab):
    def terms(p, low):
        high = forward(jnp.where(inside(p + 1, slab), fext[p + 1], 0.0))
        scales = (-ONE, -ONE, -TWO, -ONE, -TWO, -TWO, -THREE)
        for k, (term, scale) in enumerate(zip(cell_terms(low, high), scales)):
            hu[p, k] = term * scale
        return high

    lax.fori_loop(0, DEPTH, terms, forward(fext[0]))


def spread_residual(res_row, lane_row, lane_res):
    def spread(j, carry):
        value = jnp.broadcast_to(res_row[j], (NX, NX))
        at = jnp.broadcast_to(lane_row[j], (NX, NX))
        lane_id = lax.broadcasted_iota(jnp.int32, (NX, NX), 0).astype(F32)
        value = jnp.where(at == lane_id, value, 0.0)
        high = value.astype(jnp.bfloat16)
        columns = pl.ds(pl.multiple_of(j * NX, NX), NX)
        lane_res[0:NX, columns] = high
        lane_res[NX:, columns] = (value - high.astype(F32)).astype(jnp.bfloat16)
        return carry

    lax.fori_loop(0, IDX, spread, 0)


def scatter(row_hot, lane_res, invd, resid):
    def product(q, carry):
        span = pl.ds(pl.multiple_of(q * (BLOCK * NY), BLOCK * NY), BLOCK * NY)
        both = lax.dot_general(
            row_hot[span, :], lane_res[...], (((1,), (1,)), ((), ())), preferred_element_type=F32
        )
        rhs = (both[:, :NX] + both[:, NX:]).reshape(BLOCK, NY, NX)
        planes = pl.ds(q * BLOCK, BLOCK)
        resid[planes] = rhs * invd[planes]
        return carry

    lax.fori_loop(0, PLANES // BLOCK, product, 0)


def solve(coef, diag, invd, cinv, resid, direct, work, pe, lam):
    def first_step(p, applied):
        r = resid[p]
        r1 = r - (applied * (1.0 / THETA)) * invd[p]
        d2 = (ALPHA / THETA) * r + BETA * r1
        resid[p] = r1
        direct[p] = d2
        lam[p] = r * (1.0 / THETA) + d2

    apply_planes(resid, coef, 1, 13, first_step)

    def second_step(p, applied):
        r2 = resid[p] - applied * invd[p]
        resid[p] = r2
        f = diag[p] * r2
        f = f + 0.5 * (prev_x(f) + next_x(f))
        work[p] = f + 0.5 * (prev_y(f) + next_y(f))

    apply_planes(direct, coef, 2, 12, second_step)

    def correct(j):
        p = 2 * j + 3
        c = (work[p] + 0.5 * (work[p - 1] + work[p + 1])) * cinv[j]
        c = c + 0.5 * (prev_y(c) + next_y(c))
        return c + 0.5 * (prev_x(c) + next_x(c))

    def prolong(j, below):
        c = correct(j)
        pe[2 * j + 3] = c
        pe[2 * j + 2] = 0.5 * (below + c)
        return c

    first = correct(0)
    pe[3] = first
    lax.fori_loop(1, 5, prolong, first)

    def third_step(p, applied):
        r3 = resid[p] - applied * invd[p]
        resid[p] = r3
        lam[p] = lam[p] + pe[p] + r3 * (1.0 / THETA)

    apply_planes(pe, coef, 4, 10, third_step)

    def fourth_step(p, applied):
        r3 = resid[p]
        r4 = r3 - (applied * (1.0 / THETA)) * invd[p]
        lam[p] = lam[p] + (ALPHA / THETA) * r3 + BETA * r4

    apply_planes(resid, coef, 5, 9, fourth_step)


def cell_products(lam, hu, chunks):
    low = forward(lam[BELOW])
    for p in range(DEPTH):
        high = forward(lam[BELOW + p + 1])
        total = None
        for k, term in enumerate(cell_terms(low, high)):
            piece = term * hu[p, k]
            total = piece if total is None else total + piece
        low = high
        for z in range(8):
            for c in range(2):
                at = 4 * z + 2 * c
                chunks[c, z, 2 * p : 2 * p + 2, :] = total[at : at + 2, :]


def kernel(
    cond_hbm, field_hbm, pairs_hbm, obs_hbm,
    grad_ref, misfit_ref,
    cext, fext, pairs, obs, index, target,
    part, recv_xy, zsum, recv_z,
    place_row, lane_row, res_row, row_hot, lane_res, coef, diag, invd, cinv, hu,
    resid, direct, work, lam, pe,
    mis, recv_mis, chunks, recv_core, merged, recv_src,
    in_sem, send_sem, halo_sem, xy_sem, z_sem, mis_sem, core_sem, src_sem,
):
    src = lax.axis_index("src")
    slab = lax.axis_index("slab")
    zl, core = src // 2, src % 2
    zh, px, py = slab // 16, (slab // 4) % 4, slab % 4
    here = px * 4 + py
    plane_peers = [
        (src, zh * 16 + ((px + i) % 4) * 4 + (py + j) % 4)
        for i in range(4)
        for j in range(4)
        if i + j
    ]
    z_peer = (src, (1 - zh) * 16 + px * 4 + py)
    ups = [(src, (slab + k) % 32) for k in (1, 2)]
    downs = [(src, (slab + 32 - k) % 32) for k in (1, 2)]
    src_peers = [(((zl + i) % 8) * 2 + (core + j) % 2, slab) for i in range(8) for j in range(2) if i + j]
    sibling = (zl * 2 + 1 - core, slab)
    run_peers = [(zl + i) % 8 for i in range(1, 8)]

    barrier = pltpu.get_barrier_semaphore()
    greeted = plane_peers + [z_peer] + ups + downs + src_peers
    for peer in greeted:
        pl.semaphore_signal(barrier, inc=1, device_id=peer, device_id_type=MESH)

    loads = [
        pltpu.make_async_copy(pairs_hbm, pairs, in_sem.at[0]),
        pltpu.make_async_copy(field_hbm, fext.at[pl.ds(0, DEPTH)], in_sem.at[1]),
        pltpu.make_async_copy(cond_hbm, cext.at[pl.ds(6, DEPTH)], in_sem.at[2]),
        pltpu.make_async_copy(obs_hbm, obs, in_sem.at[3]),
    ]
    for load in loads:
        load.start()
    loads[0].wait()
    read_pairs(pairs, index, place_row, lane_row, slab)
    loads[1].wait()
    gather(fext, index, part, slab)
    recv_xy[here] = part[...]
    loads[2].wait()

    sent = []

    def send(source, dest, arrival, peer):
        copy = pltpu.make_async_remote_copy(
            src_ref=source, dst_ref=dest, send_sem=send_sem, recv_sem=arrival,
            device_id=peer, device_id_type=MESH,
        )
        copy.start()
        sent.append(copy)

    def arrived(buffer, arrival):
        pltpu.make_async_copy(buffer, buffer, arrival).wait()

    pl.semaphore_wait(barrier, len(greeted))
    for peer in plane_peers:
        send(part, recv_xy.at[here], xy_sem, peer)
    own = cext.at[pl.ds(6, DEPTH)]
    send(own, cext.at[pl.ds(2, DEPTH)], halo_sem.at[0], ups[0])
    send(own, cext.at[pl.ds(10, DEPTH)], halo_sem.at[1], downs[0])
    send(cext.at[pl.ds(8, 2)], cext.at[pl.ds(0, 2)], halo_sem.at[2], ups[1])
    send(cext.at[pl.ds(6, 2)], cext.at[pl.ds(14, 2)], halo_sem.at[3], downs[1])
    send(fext.at[pl.ds(0, 1)], fext.at[pl.ds(DEPTH, 1)], halo_sem.at[4], downs[0])
    loads[3].wait()
    read_target(obs, target, src)
    one_hot_rows(place_row, row_hot)

    arrived(recv_xy.at[pl.ds(0, 15)], xy_sem)
    zsum[...] = lax.fori_loop(1, 16, lambda k, acc: acc + recv_xy[k], recv_xy[0])
    send(zsum, recv_z, z_sem, z_peer)

    arrived(cext.at[pl.ds(2, DEPTH)], halo_sem.at[0])
    arrived(cext.at[pl.ds(10, DEPTH)], halo_sem.at[1])
    arrived(cext.at[pl.ds(0, 2)], halo_sem.at[2])
    arrived(cext.at[pl.ds(14, 2)], halo_sem.at[3])
    arrived(fext.at[pl.ds(DEPTH, 1)], halo_sem.at[4])
    conductivity_terms(cext, coef, diag, invd, cinv, slab)
    field_terms(fext, hu, slab)

    arrived(recv_z, z_sem)
    res = (zsum[...] + recv_z[...]) - target[...]
    for j in range(RROWS):
        res_row[j] = res[j : j + 1, :]
        res_row[RROWS + j] = -res[j : j + 1, :]
    half = jnp.sum(jnp.sum(0.5 * res * res, axis=0, keepdims=True), axis=1, keepdims=True)
    mis[...] = jnp.broadcast_to(half, (1, NX))
    recv_mis[src] = mis[...]
    for peer in src_peers:
        send(mis, recv_mis.at[src], mis_sem, peer)

    spread_residual(res_row, lane_row, lane_res)
    scatter(row_hot, lane_res, invd, resid)
    solve(coef, diag, invd, cinv, resid, direct, work, pe, lam)
    cell_products(lam, hu, chunks)

    send(chunks.at[1 - core], recv_core, core_sem, sibling)
    arrived(recv_core, core_sem)
    merged[...] = chunks[core] + recv_core[...]
    for z in run_peers:
        send(merged.at[z], recv_src.at[zl], src_sem, (z * 2 + core, slab))
    recv_src[zl] = merged[zl]
    arrived(recv_mis.at[pl.ds(0, 15)], mis_sem)
    misfit = recv_mis[0]
    for k in range(1, GROUPS):
        misfit = misfit + recv_mis[k]
    misfit_ref[...] = misfit * (1.0 / (GROUPS * RX))
    arrived(recv_src.at[pl.ds(0, 7)], src_sem)
    total = recv_src[0]
    for k in range(1, 8):
        total = total + recv_src[k]
    grad_ref[...] = total
    for copy in sent:
        copy.wait_send()


def on_device(conductivity, forward_fields, receiver_pairs, observed):
    field = forward_fields.reshape(DEPTH, NY, NX)
    pairs = jnp.transpose(receiver_pairs[0])
    conductivity, field, pairs, observed = (
        pltpu.with_memory_space_constraint(a, pltpu.HBM) for a in (conductivity, field, pairs, observed)
    )
    plane = (NY, NX)
    any_spec = pl.BlockSpec(memory_space=pltpu.HBM)
    vmem = pl.BlockSpec(memory_space=pltpu.VMEM)
    dma = pltpu.SemaphoreType.DMA
    grad, misfit = pl.pallas_call(
        kernel,
        name="adjoint_gradient",
        out_shape=(jax.ShapeDtypeStruct((8, NX), F32), jax.ShapeDtypeStruct((1, NX), F32)),
        in_specs=[any_spec] * 4,
        out_specs=(vmem, vmem),
        scratch_shapes=[
            pltpu.VMEM((CELLS, *plane), F32),
            pltpu.VMEM((DEPTH + 1, *plane), F32),
            pltpu.VMEM((2, RX), jnp.int32),
            pltpu.VMEM((GROUPS, RX), F32),
            pltpu.VMEM((IDX, NX), jnp.int32),
            pltpu.VMEM((RROWS, NX), F32),
            pltpu.VMEM((RROWS, NX), F32),
            pltpu.VMEM((16, RROWS, NX), F32),
            pltpu.VMEM((RROWS, NX), F32),
            pltpu.VMEM((RROWS, NX), F32),
            pltpu.VMEM((IDX, 1, NX), F32),
            pltpu.VMEM((IDX, 1, NX), F32),
            pltpu.VMEM((IDX, 1, NX), F32),
            pltpu.VMEM((PLANES * NY, IDX * NX), jnp.bfloat16),
            pltpu.VMEM((2 * NX, IDX * NX), jnp.bfloat16),
            pltpu.VMEM((3, PLANES, *plane), F32),
            pltpu.VMEM((PLANES, *plane), F32),
            pltpu.VMEM((PLANES, *plane), F32),
            pltpu.VMEM((5, *plane), F32),
            pltpu.VMEM((DEPTH, 7, *plane), F32),
            pltpu.VMEM((PLANES, *plane), F32),
            pltpu.VMEM((PLANES, *plane), F32),
            pltpu.VMEM((PLANES, *plane), F32),
            pltpu.VMEM((PLANES, *plane), F32),
            pltpu.VMEM((PLANES, *plane), F32),
            pltpu.VMEM((1, NX), F32),
            pltpu.VMEM((GROUPS, 1, NX), F32),
            pltpu.VMEM((2, 8, 8, NX), F32),
            pltpu.VMEM((8, 8, NX), F32),
            pltpu.VMEM((8, 8, NX), F32),
            pltpu.VMEM((8, 8, NX), F32),
            dma((4,)), dma, dma((5,)), dma, dma, dma, dma, dma,
        ],
        compiler_params=pltpu.CompilerParams(
            collective_id=0, has_side_effects=True, vmem_limit_bytes=32 * 1024 * 1024
        ),
    )(conductivity, field, pairs, observed)
    return grad.reshape(DEPTH, 2, NX), misfit[0, 0]


def solution(mesh):
    in_specs = (P("slab", None, None), P("src", "slab", None, None), P("src", None, None), P())
    out_specs = (P("slab", "src", None), P())
    return jax.shard_map(
        on_device, mesh=mesh, in_specs=in_specs, out_specs=out_specs, check_vma=False
    )
```

time: 64.1 us -> 48.4 us (0.76)
  Pallas kernels: 58.1 us -> 45.9 us
  local copies, waits for them, and re-layouts: 3.89 us -> 0.6 us
    pallas_call x1, Pallas kernels: 58.1 us -> 45.9 us  [on_device(): pl.pallas_call(kernel, name='adjoint_gradient', out_shape=(jax.ShapeDtype...]
    unnamed x9 -> x1, local copies, waits for them, and re-layouts: 3.89 us -> 0.6 us
where the time goes in v2:
time: 48.4 us; the launch traced here: 48.3 us
  Pallas kernels  45.9 us (95%)
  between operations  1.8 us (4%)
  local copies, waits for them, and re-layouts  0.6 us (1%)
    pallas_call x1, Pallas kernels, on_device(): pl.pallas_call(kernel, name='adjoint_gradient', out_shape=(jax.ShapeDtype...  45.9 us

profile of v2, /device:TPU:1, one launch (start us, length us, event | category | flops | bytes accessed | tf_op | source)
XLA Modules:
  0.0 48.3 jit_solution(15276545091276147171)
XLA Ops:
  0.6 45.9 %adjoint_gradient.1 = (f32[8,128]{1,0:T(8,128)S(1)}, f32[1,128]{1,0:T(1,128)S(1)}) custom-call(f32[4,32,128]{2,1,0:T(8,128)} %cond_hbm.1, f32[4,32,128]{2,1,0:T(8,128)} %bitcast.9, s32[2,2000]{1,0:T(2,128)} %bitcast.10, f32[16,2000]{1,0:T(8,128)} %obs_hbm.1), custom_call_target="tpu_custom_call" | custom-call | tf_op jit(solution)/shard_map/adjoint_gradient/pallas_call | solution.py:448
  46.5 0.6 %copy.8 = f32[4,2,128]{2,1,0:T(2,128)} copy(f32[4,2,128]{2,1,0:T(2,128)S(1)} %bitcast.7) | data formatting | bytes 8192

commit v3 on v2

--- a/solution.py
+++ b/solution.py
@@ -28,6 +28,7 @@
 RROWS = 16
 IDX = 2 * RROWS
 GROUPS = 16
+CROSSING = ((14, 16), (15, 16), (15, 17))
 NZ = 128
 MESH = pl.DeviceIdType.MESH
 F32 = jnp.float32
@@ -147,15 +148,17 @@
             acc = jnp.where(line == block * 8 + k, found, acc)
         return acc
 
-    picked = lax.fori_loop(0, DEPTH * NY // 8, pick, jnp.zeros((IDX, NX), F32))
+    picked = lax.fori_loop(0, DEPTH * NY // 8, pick, jnp.zeros((IDX, NX), F32), unroll=True)
     part[...] = picked[:RROWS] - picked[RROWS:]
 
 
-def one_hot_rows(place_row, row_hot):
+def one_hots(place_row, lane_row, row_hot, lane_hot):
     def hot(j, carry):
-        spread = jnp.broadcast_to(place_row[j], (PLANES * NY, NX))
-        line_id = lax.broadcasted_iota(jnp.int32, (PLANES * NY, NX), 0).astype(F32)
-        row_hot[:, pl.ds(pl.multiple_of(j * NX, NX), NX)] = jnp.where(spread == line_id, 1.0, 0.0).astype(jnp.bfloat16)
+        columns = pl.ds(pl.multiple_of(j * NX, NX), NX)
+        for at, out, size in ((place_row, row_hot, PLANES * NY), (lane_row, lane_hot, NX)):
+            spread = jnp.broadcast_to(at[j], (size, NX))
+            line_id = lax.broadcasted_iota(jnp.int32, (size, NX), 0).astype(F32)
+            out[:, columns] = jnp.where(spread == line_id, 1.0, 0.0).astype(jnp.bfloat16)
         return carry
 
     lax.fori_loop(0, IDX, hot, 0)
@@ -186,7 +189,7 @@
         invd[p] = jnp.where(keep, 1.0 / jnp.where(keep, value, 1.0), 0.0)
         return boxed
 
-    lax.fori_loop(0, PLANES, diagonals, around(masked_cells(0)))
+    lax.fori_loop(0, PLANES, diagonals, around(masked_cells(0)), unroll=5)
 
     even = jnp.logical_and(lanes() % 2 == 0, rows() % 2 == 0)
 
@@ -204,7 +207,7 @@
         cinv[j - 1] = jnp.where(keep, OMEGA / jnp.where(keep, value, 1.0), 0.0)
         return boxed
 
-    lax.fori_loop(1, 6, coarse, coarse_box(0))
+    lax.fori_loop(1, 6, coarse, coarse_box(0), unroll=True)
 
 
 def field_terms(fext, hu, slab):
@@ -215,22 +218,21 @@
             hu[p, k] = term * scale
         return high
 
-    lax.fori_loop(0, DEPTH, terms, forward(fext[0]))
-
-
-def spread_residual(res_row, lane_row, lane_res):
+    lax.fori_loop(0, DEPTH, terms, forward(fext[0]), unroll=True)
+
+
+def spread_residual(res_row, lane_hot, lane_res):
     def spread(j, carry):
-        value = jnp.broadcast_to(res_row[j], (NX, NX))
-        at = jnp.broadcast_to(lane_row[j], (NX, NX))
-        lane_id = lax.broadcasted_iota(jnp.int32, (NX, NX), 0).astype(F32)
-        value = jnp.where(at == lane_id, value, 0.0)
+        columns = pl.ds(pl.multiple_of(j * NX, NX), NX)
+        value = jnp.broadcast_to(res_row[j], (16, NX))
         high = value.astype(jnp.bfloat16)
-        columns = pl.ds(pl.multiple_of(j * NX, NX), NX)
-        lane_res[0:NX, columns] = high
-        lane_res[NX:, columns] = (value - high.astype(F32)).astype(jnp.bfloat16)
+        low = (value - high.astype(F32)).astype(jnp.bfloat16)
+        hot = lane_hot[:, columns].reshape(NX // 16, 16, NX)
+        lane_res[0:NX, columns] = (hot * high[None]).reshape(NX, NX)
+        lane_res[NX:, columns] = (hot * low[None]).reshape(NX, NX)
         return carry
 
-    lax.fori_loop(0, IDX, spread, 0)
+    lax.fori_loop(0, IDX, spread, 0, unroll=4)
 
 
 def scatter(row_hot, lane_res, invd, resid):
@@ -281,7 +283,7 @@
 
     first = correct(0)
     pe[3] = first
-    lax.fori_loop(1, 5, prolong, first)
+    lax.fori_loop(1, 5, prolong, first, unroll=True)
 
     def third_step(p, applied):
         r3 = resid[p] - applied * invd[p]
@@ -315,13 +317,14 @@
 
 def kernel(
     cond_hbm, field_hbm, pairs_hbm, obs_hbm,
-    grad_ref, misfit_ref,
+    recv_src, recv_mis,
     cext, fext, pairs, obs, index, target,
     part, recv_xy, zsum, recv_z,
-    place_row, lane_row, res_row, row_hot, lane_res, coef, diag, invd, cinv, hu,
+    place_row, lane_row, res_row, row_hot, lane_hot, lane_res, coef, diag, invd, cinv, hu,
     resid, direct, work, lam, pe,
-    mis, recv_mis, chunks, recv_core, merged, recv_src,
+    mis, mis_core, mis_sum, chunks, recv_core, merged,
     in_sem, send_sem, halo_sem, xy_sem, z_sem, mis_sem, core_sem, src_sem,
+    ready_z, ready_halo, ready_core, ready_src,
 ):
     src = lax.axis_index("src")
     slab = lax.axis_index("slab")
@@ -334,17 +337,9 @@
         for j in range(4)
         if i + j
     ]
-    z_peer = (src, (1 - zh) * 16 + px * 4 + py)
-    ups = [(src, (slab + k) % 32) for k in (1, 2)]
-    downs = [(src, (slab + 32 - k) % 32) for k in (1, 2)]
-    src_peers = [(((zl + i) % 8) * 2 + (core + j) % 2, slab) for i in range(8) for j in range(2) if i + j]
+    z_peer = (src, (1 - zh) * 16 + here)
     sibling = (zl * 2 + 1 - core, slab)
-    run_peers = [(zl + i) % 8 for i in range(1, 8)]
-
-    barrier = pltpu.get_barrier_semaphore()
-    greeted = plane_peers + [z_peer] + ups + downs + src_peers
-    for peer in greeted:
-        pl.semaphore_signal(barrier, inc=1, device_id=peer, device_id_type=MESH)
+    low_half, high_half = zh == 0, zh == 1
 
     loads = [
         pltpu.make_async_copy(pairs_hbm, pairs, in_sem.at[0]),
@@ -354,50 +349,139 @@
     ]
     for load in loads:
         load.start()
+
+    barrier = pltpu.get_barrier_semaphore()
+
+    def signal(sem, peer):
+        pl.semaphore_signal(sem, inc=1, device_id=peer, device_id_type=MESH)
+
+    for peer in plane_peers:
+        signal(barrier, peer)
+
+    @pl.when(low_half)
+    def _():
+        signal(barrier, z_peer)
+
+    for at, to in CROSSING:
+
+        @pl.when(slab == at)
+        def _():
+            signal(barrier, (src, to))
+
+    for z in range(8):
+        after = jnp.where(low_half, z > zl, z < zl)
+
+        @pl.when(after)
+        def _():
+            signal(barrier, (z * 2 + core, slab))
+
+    @pl.when(core == 1)
+    def _():
+        signal(barrier, sibling)
+
     loads[0].wait()
     read_pairs(pairs, index, place_row, lane_row, slab)
     loads[1].wait()
     gather(fext, index, part, slab)
     recv_xy[here] = part[...]
-    loads[2].wait()
 
     sent = []
 
-    def send(source, dest, arrival, peer):
+    def send(source, dest, arrival, peer, when=None):
         copy = pltpu.make_async_remote_copy(
             src_ref=source, dst_ref=dest, send_sem=send_sem, recv_sem=arrival,
             device_id=peer, device_id_type=MESH,
         )
-        copy.start()
-        sent.append(copy)
+        sent.append((copy.wait_send, when))
+        if when is None:
+            copy.start()
+        else:
+            pl.when(when)(copy.start)
 
     def arrived(buffer, arrival):
         pltpu.make_async_copy(buffer, buffer, arrival).wait()
 
-    pl.semaphore_wait(barrier, len(greeted))
+    def wait_for(sem, count):
+        @pl.when(count > 0)
+        def _():
+            pl.semaphore_wait(sem, count)
+
+    def number(flag):
+        return flag.astype(jnp.int32)
+
+    crossed = sum(number(slab == to) for _, to in CROSSING)
+    crossing = sum(number(slab == at) for at, _ in CROSSING)
+    before = jnp.where(low_half, zl, 7 - zl)
+    pl.semaphore_wait(barrier, 15 + zh + crossed + before + (1 - core))
     for peer in plane_peers:
         send(part, recv_xy.at[here], xy_sem, peer)
+
+    @pl.when(high_half)
+    def _():
+        signal(ready_z, z_peer)
+
+    for at, to in CROSSING:
+
+        @pl.when(slab == to)
+        def _():
+            signal(ready_halo, (src, at))
+
+    for z in range(8):
+        earlier = jnp.where(low_half, z < zl, z > zl)
+
+        @pl.when(earlier)
+        def _():
+            signal(ready_src, (z * 2 + core, slab))
+
+    @pl.when(core == 0)
+    def _():
+        signal(ready_core, sibling)
+
+    loads[2].wait()
     own = cext.at[pl.ds(6, DEPTH)]
-    send(own, cext.at[pl.ds(2, DEPTH)], halo_sem.at[0], ups[0])
-    send(own, cext.at[pl.ds(10, DEPTH)], halo_sem.at[1], downs[0])
-    send(cext.at[pl.ds(8, 2)], cext.at[pl.ds(0, 2)], halo_sem.at[2], ups[1])
-    send(cext.at[pl.ds(6, 2)], cext.at[pl.ds(14, 2)], halo_sem.at[3], downs[1])
-    send(fext.at[pl.ds(0, 1)], fext.at[pl.ds(DEPTH, 1)], halo_sem.at[4], downs[0])
+    own_low, own_high = cext.at[pl.ds(6, 2)], cext.at[pl.ds(8, 2)]
+    at_1, at_2 = slab == 15, jnp.logical_or(slab == 14, slab == 15)
+    up_1 = (own, cext.at[pl.ds(2, DEPTH)], halo_sem.at[0], (src, (slab + 1) % 32))
+    up_2 = (own_high, cext.at[pl.ds(0, 2)], halo_sem.at[2], (src, (slab + 2) % 32))
+    down_1, down_2 = (src, (slab + 31) % 32), (src, (slab + 30) % 32)
+    send(own, cext.at[pl.ds(10, DEPTH)], halo_sem.at[1], down_1, slab > 0)
+    send(fext.at[pl.ds(0, 1)], fext.at[pl.ds(DEPTH, 1)], halo_sem.at[4], down_1, slab > 0)
+    send(own_low, cext.at[pl.ds(14, 2)], halo_sem.at[3], down_2, slab > 1)
+    send(*up_1, jnp.logical_and(slab < 31, jnp.logical_not(at_1)))
+    send(*up_2, jnp.logical_and(slab < 30, jnp.logical_not(at_2)))
     loads[3].wait()
     read_target(obs, target, src)
-    one_hot_rows(place_row, row_hot)
+    one_hots(place_row, lane_row, row_hot, lane_hot)
 
     arrived(recv_xy.at[pl.ds(0, 15)], xy_sem)
-    zsum[...] = lax.fori_loop(1, 16, lambda k, acc: acc + recv_xy[k], recv_xy[0])
+    zsum[...] = lax.fori_loop(1, 16, lambda k, acc: acc + recv_xy[k], recv_xy[0], unroll=True)
+    wait_for(ready_z, 1 - zh)
     send(zsum, recv_z, z_sem, z_peer)
-
-    arrived(cext.at[pl.ds(2, DEPTH)], halo_sem.at[0])
-    arrived(cext.at[pl.ds(10, DEPTH)], halo_sem.at[1])
-    arrived(cext.at[pl.ds(0, 2)], halo_sem.at[2])
-    arrived(cext.at[pl.ds(14, 2)], halo_sem.at[3])
-    arrived(fext.at[pl.ds(DEPTH, 1)], halo_sem.at[4])
+    wait_for(ready_halo, crossing)
+    send(*up_1, at_1)
+    send(*up_2, at_2)
+
+    @pl.when(slab > 0)
+    def _():
+        arrived(cext.at[pl.ds(2, DEPTH)], halo_sem.at[0])
+
+    @pl.when(slab > 1)
+    def _():
+        arrived(cext.at[pl.ds(0, 2)], halo_sem.at[2])
+
+    @pl.when(slab < 31)
+    def _():
+        arrived(cext.at[pl.ds(10, DEPTH)], halo_sem.at[1])
+        arrived(fext.at[pl.ds(DEPTH, 1)], halo_sem.at[4])
+
+    @pl.when(slab < 30)
+    def _():
+        arrived(cext.at[pl.ds(14, 2)], halo_sem.at[3])
+
     conductivity_terms(cext, coef, diag, invd, cinv, slab)
     field_terms(fext, hu, slab)
+    wait_for(ready_core, core)
+    wait_for(ready_src, 7 - before)
 
     arrived(recv_z, z_sem)
     res = (zsum[...] + recv_z[...]) - target[...]
@@ -406,33 +490,43 @@
         res_row[RROWS + j] = -res[j : j + 1, :]
     half = jnp.sum(jnp.sum(0.5 * res * res, axis=0, keepdims=True), axis=1, keepdims=True)
     mis[...] = jnp.broadcast_to(half, (1, NX))
-    recv_mis[src] = mis[...]
-    for peer in src_peers:
-        send(mis, recv_mis.at[src], mis_sem, peer)
-
-    spread_residual(res_row, lane_row, lane_res)
+    send(mis, mis_core, mis_sem.at[0], sibling)
+
+    spread_residual(res_row, lane_hot, lane_res)
     scatter(row_hot, lane_res, invd, resid)
+
+    arrived(mis_core, mis_sem.at[0])
+    mis_sum[...] = mis[...] + mis_core[...]
+    recv_mis[zl] = mis_sum[...]
+    for k in range(1, 8):
+        z = (zl + k) % 8
+        send(mis_sum, recv_mis.at[zl], mis_sem.at[1], (z * 2 + core, slab))
+
     solve(coef, diag, invd, cinv, resid, direct, work, pe, lam)
     cell_products(lam, hu, chunks)
 
     send(chunks.at[1 - core], recv_core, core_sem, sibling)
     arrived(recv_core, core_sem)
     merged[...] = chunks[core] + recv_core[...]
-    for z in run_peers:
+    for k in range(1, 8):
+        z = (zl + k) % 8
         send(merged.at[z], recv_src.at[zl], src_sem, (z * 2 + core, slab))
     recv_src[zl] = merged[zl]
-    arrived(recv_mis.at[pl.ds(0, 15)], mis_sem)
-    misfit = recv_mis[0]
-    for k in range(1, GROUPS):
-        misfit = misfit + recv_mis[k]
+    arrived(recv_mis.at[pl.ds(0, 7)], mis_sem.at[1])
+    arrived(recv_src.at[pl.ds(0, 7)], src_sem)
+    for wait, when in sent:
+        if when is None:
+            wait()
+        else:
+            pl.when(when)(wait)
+
+
+def finish(recv_src, recv_mis, grad_ref, misfit_ref):
+    total, misfit = recv_src[0], recv_mis[0]
+    for k in range(1, 8):
+        total, misfit = total + recv_src[k], misfit + recv_mis[k]
+    grad_ref[...] = total
     misfit_ref[...] = misfit * (1.0 / (GROUPS * RX))
-    arrived(recv_src.at[pl.ds(0, 7)], src_sem)
-    total = recv_src[0]
-    for k in range(1, 8):
-        total = total + recv_src[k]
-    grad_ref[...] = total
-    for copy in sent:
-        copy.wait_send()
 
 
 def on_device(conductivity, forward_fields, receiver_pairs, observed):
@@ -444,11 +538,14 @@
     plane = (NY, NX)
     any_spec = pl.BlockSpec(memory_space=pltpu.HBM)
     vmem = pl.BlockSpec(memory_space=pltpu.VMEM)
-    dma = pltpu.SemaphoreType.DMA
-    grad, misfit = pl.pallas_call(
+    dma, regular = pltpu.SemaphoreType.DMA, pltpu.SemaphoreType.REGULAR
+    received = pl.pallas_call(
         kernel,
         name="adjoint_gradient",
-        out_shape=(jax.ShapeDtypeStruct((8, NX), F32), jax.ShapeDtypeStruct((1, NX), F32)),
+        out_shape=(
+            jax.ShapeDtypeStruct((8, 8, NX), F32),
+            jax.ShapeDtypeStruct((8, 1, NX), F32),
+        ),
         in_specs=[any_spec] * 4,
         out_specs=(vmem, vmem),
         scratch_shapes=[
@@ -466,6 +563,7 @@
             pltpu.VMEM((IDX, 1, NX), F32),
             pltpu.VMEM((IDX, 1, NX), F32),
             pltpu.VMEM((PLANES * NY, IDX * NX), jnp.bfloat16),
+            pltpu.VMEM((NX, IDX * NX), jnp.bfloat16),
             pltpu.VMEM((2 * NX, IDX * NX), jnp.bfloat16),
             pltpu.VMEM((3, PLANES, *plane), F32),
             pltpu.VMEM((PLANES, *plane), F32),
@@ -478,17 +576,25 @@
             pltpu.VMEM((PLANES, *plane), F32),
             pltpu.VMEM((PLANES, *plane), F32),
             pltpu.VMEM((1, NX), F32),
-            pltpu.VMEM((GROUPS, 1, NX), F32),
+            pltpu.VMEM((1, NX), F32),
+            pltpu.VMEM((1, NX), F32),
             pltpu.VMEM((2, 8, 8, NX), F32),
             pltpu.VMEM((8, 8, NX), F32),
             pltpu.VMEM((8, 8, NX), F32),
-            pltpu.VMEM((8, 8, NX), F32),
-            dma((4,)), dma, dma((5,)), dma, dma, dma, dma, dma,
+            dma((4,)), dma, dma((5,)), dma, dma, dma((2,)), dma, dma,
+            regular, regular, regular, regular,
         ],
         compiler_params=pltpu.CompilerParams(
             collective_id=0, has_side_effects=True, vmem_limit_bytes=32 * 1024 * 1024
         ),
     )(conductivity, field, pairs, observed)
+    grad, misfit = pl.pallas_call(
+        finish,
+        name="add_groups",
+        out_shape=(jax.ShapeDtypeStruct((8, NX), F32), jax.ShapeDtypeStruct((1, NX), F32)),
+        in_specs=[vmem] * 2,
+        out_specs=(vmem, vmem),
+    )(*received)
     return grad.reshape(DEPTH, 2, NX), misfit[0, 0]
 
 

time: 48.4 us -> 47.1 us (0.973)
  between operations: 1.8 us -> 0.65 us
  Pallas kernels: 45.9 us -> 45.1 us
  local copies, waits for them, and re-layouts: 0.6 us -> 1.19 us
    pallas_call x1, Pallas kernels: 45.9 us -> 43.7 us  [on_device(): pl.pallas_call(kernel, name='adjoint_gradient', out_shape=(jax.ShapeDtype...]
    pallas_call x0 -> x1, Pallas kernels: none -> 1.36 us  [on_device(): pl.pallas_call(finish, name='add_groups', out_shape=(jax.ShapeDtypeStruct...]
    unnamed x1 -> x4, local copies, waits for them, and re-layouts: 0.6 us -> 1.19 us
where the time goes in v3:
time: 47.1 us; the launch traced here: 46.9 us
  Pallas kernels  45.1 us (96%)
  local copies, waits for them, and re-layouts  1.19 us (3%)
  between operations  0.65 us (1%)
    pallas_call x1, Pallas kernels, on_device(): pl.pallas_call(kernel, name='adjoint_gradient', out_shape=(jax.ShapeDtype...  43.7 us
    pallas_call x1, Pallas kernels, on_device(): pl.pallas_call(finish, name='add_groups', out_shape=(jax.ShapeDtypeStruct...  1.36 us
    unnamed x4, local copies, waits for them, and re-layouts  1.19 us

profile of v3, /device:TPU:1, one launch (start us, length us, event | category | flops | bytes accessed | tf_op | source)
XLA Modules:
  0.0 46.9 jit_solution(13537419644636816808)
XLA Ops:
  0.6 43.7 %adjoint_gradient.1 = (f32[8,8,128]{2,1,0:T(8,128)S(1)}, f32[8,1,128]{2,1,0:T(1,128)S(1)}) custom-call(f32[4,32,128]{2,1,0:T(8,128)} %cond_hbm.1, f32[4,32,128]{2,1,0:T(8,128)} %bitcast.7, s32[2,2000]{1,0:T(2,128)} %bitcast.8, f32[16,2000]{1,0:T(8,128)} %obs_hbm.1), custom_call_target="tpu_custom_call" | custom-call | tf_op jit(solution)/shard_map/adjoint_gradient/pallas_call | solution.py:542
  44.4 0.0 copy-start
  44.4 0.6 %copy-done = f32[8,8,128]{2,1,0:T(8,128)} copy-done((f32[8,8,128]{2,1,0:T(8,128)}, f32[8,8,128]{2,1,0:T(8,128)S(1)}, u32[]{:S(2)}) %copy-start) | copy-done | bytes 32792
  45.0 0.0 copy-start.1
  45.0 0.6 %copy-done.1 = f32[8,1,128]{2,1,0:T(1,128)} copy-done((f32[8,1,128]{2,1,0:T(1,128)}, f32[8,1,128]{2,1,0:T(1,128)S(1)}, u32[]{:S(2)}) %copy-start.1) | copy-done | bytes 4120
  45.5 1.4 %add_groups.1 = (f32[8,128]{1,0:T(8,128)}, f32[1,128]{1,0:T(1,128)}) custom-call(f32[8,8,128]{2,1,0:T(8,128)} %copy-done, f32[8,1,128]{2,1,0:T(1,128)} %copy-done.1), custom_call_target="tpu_custom_call" | custom-call | tf_op jit(solution)/shard_map/add_groups/pallas_call | solution.py:591
Async XLA Ops:
  44.4 0.6 %copy-start = (f32[8,8,128]{2,1,0:T(8,128)}, f32[8,8,128]{2,1,0:T(8,128)S(1)}, u32[]{:S(2)}) copy-start(f32[8,8,128]{2,1,0:T(8,128)S(1)} %get-tuple-element.6.recv_src) | copy-start | bytes 98308
  45.0 0.6 %copy-start.1 = (f32[8,1,128]{2,1,0:T(1,128)}, f32[8,1,128]{2,1,0:T(1,128)S(1)}, u32[]{:S(2)}) copy-start(f32[8,1,128]{2,1,0:T(1,128)S(1)} %get-tuple-element.7.recv_mis) | copy-start | bytes 12292

commit v4 on v3

--- a/solution.py
+++ b/solution.py
@@ -28,6 +28,8 @@
 RROWS = 16
 IDX = 2 * RROWS
 GROUPS = 16
+UPWARD = ((14, 16, 8, 0, 0), (15, 16, 6, 2, 1), (15, 16, 8, 4, 2), (15, 17, 8, 0, 0))
+DOWNWARD = ((16, 15, 6, 10, 0), (16, 15, 8, 12, 1), (17, 15, 6, 14, 2), (16, 14, 6, 14, 0))
 CROSSING = ((14, 16), (15, 16), (15, 17))
 NZ = 128
 MESH = pl.DeviceIdType.MESH
@@ -324,7 +326,7 @@
     resid, direct, work, lam, pe,
     mis, mis_core, mis_sum, chunks, recv_core, merged,
     in_sem, send_sem, halo_sem, xy_sem, z_sem, mis_sem, core_sem, src_sem,
-    ready_z, ready_halo, ready_core, ready_src,
+    cross_sem, swap_sem, ready_z, ready_halo, ready_core, ready_src, ready_field,
 ):
     src = lax.axis_index("src")
     slab = lax.axis_index("slab")
@@ -340,6 +342,13 @@
     z_peer = (src, (1 - zh) * 16 + here)
     sibling = (zl * 2 + 1 - core, slab)
     low_half, high_half = zh == 0, zh == 1
+    first = jnp.where(zl < 4, zh, 1 - zh) == 0
+    second = jnp.logical_not(first)
+    edge = jnp.logical_or(zl == 0, zl == 7)
+    beyond = (7 - zl) * 2 + core
+    greets_field = jnp.logical_and(first, jnp.logical_or(slab == 15, slab == 16))
+    hears_field = jnp.logical_and(second, jnp.logical_or(slab == 15, slab == 16))
+    across = (src, 31 - slab)
 
     loads = [
         pltpu.make_async_copy(pairs_hbm, pairs, in_sem.at[0]),
@@ -358,15 +367,19 @@
     for peer in plane_peers:
         signal(barrier, peer)
 
-    @pl.when(low_half)
+    @pl.when(first)
     def _():
         signal(barrier, z_peer)
 
     for at, to in CROSSING:
 
-        @pl.when(slab == at)
-        def _():
-            signal(barrier, (src, to))
+        @pl.when(jnp.logical_and(edge, slab == at))
+        def _():
+            signal(barrier, (beyond, to))
+
+    @pl.when(greets_field)
+    def _():
+        signal(barrier, across)
 
     for z in range(8):
         after = jnp.where(low_half, z > zl, z < zl)
@@ -409,22 +422,27 @@
     def number(flag):
         return flag.astype(jnp.int32)
 
-    crossed = sum(number(slab == to) for _, to in CROSSING)
-    crossing = sum(number(slab == at) for at, _ in CROSSING)
+    crossed = sum(number(slab == to) for _, to in CROSSING) * number(edge)
+    crossing = sum(number(slab == at) for at, _ in CROSSING) * number(edge)
     before = jnp.where(low_half, zl, 7 - zl)
-    pl.semaphore_wait(barrier, 15 + zh + crossed + before + (1 - core))
+    heard = 15 + number(second) + crossed + number(hears_field) + before + (1 - core)
+    pl.semaphore_wait(barrier, heard)
     for peer in plane_peers:
         send(part, recv_xy.at[here], xy_sem, peer)
 
-    @pl.when(high_half)
+    @pl.when(second)
     def _():
         signal(ready_z, z_peer)
 
     for at, to in CROSSING:
 
-        @pl.when(slab == to)
-        def _():
-            signal(ready_halo, (src, at))
+        @pl.when(jnp.logical_and(edge, slab == to))
+        def _():
+            signal(ready_halo, (beyond, at))
+
+    @pl.when(jnp.logical_and(hears_field, slab == 15))
+    def _():
+        signal(ready_field, across)
 
     for z in range(8):
         earlier = jnp.where(low_half, z < zl, z > zl)
@@ -438,51 +456,85 @@
         signal(ready_core, sibling)
 
     loads[2].wait()
+    def cross(blocks):
+        for at, to, take, put, k in blocks:
+            send(
+                cext.at[take + core], cext.at[put + core], cross_sem.at[k], (beyond, to),
+                jnp.logical_and(edge, slab == at),
+            )
+
     own = cext.at[pl.ds(6, DEPTH)]
     own_low, own_high = cext.at[pl.ds(6, 2)], cext.at[pl.ds(8, 2)]
-    at_1, at_2 = slab == 15, jnp.logical_or(slab == 14, slab == 15)
-    up_1 = (own, cext.at[pl.ds(2, DEPTH)], halo_sem.at[0], (src, (slab + 1) % 32))
-    up_2 = (own_high, cext.at[pl.ds(0, 2)], halo_sem.at[2], (src, (slab + 2) % 32))
+    from_1, from_2 = cext.at[pl.ds(2, DEPTH)], cext.at[pl.ds(0, 2)]
+    to_1, to_2 = cext.at[pl.ds(10, DEPTH)], cext.at[pl.ds(14, 2)]
+    up_1, up_2 = (src, (slab + 1) % 32), (src, (slab + 2) % 32)
     down_1, down_2 = (src, (slab + 31) % 32), (src, (slab + 30) % 32)
-    send(own, cext.at[pl.ds(10, DEPTH)], halo_sem.at[1], down_1, slab > 0)
-    send(fext.at[pl.ds(0, 1)], fext.at[pl.ds(DEPTH, 1)], halo_sem.at[4], down_1, slab > 0)
-    send(own_low, cext.at[pl.ds(14, 2)], halo_sem.at[3], down_2, slab > 1)
-    send(*up_1, jnp.logical_and(slab < 31, jnp.logical_not(at_1)))
-    send(*up_2, jnp.logical_and(slab < 30, jnp.logical_not(at_2)))
+
+    def among(*slabs):
+        found = slab == slabs[0]
+        for other in slabs[1:]:
+            found = jnp.logical_or(found, slab == other)
+        return found
+
+    sends_up_1, sends_up_2 = (jnp.logical_not(among(*t)) for t in ((15, 31), (14, 15, 30, 31)))
+    sends_down_1, sends_down_2 = (jnp.logical_not(among(*t)) for t in ((0, 16), (0, 1, 16, 17)))
+    top = fext.at[pl.ds(DEPTH, 1)]
+    bottom = fext.at[pl.ds(0, 1)]
+    send(own, to_1, halo_sem.at[1], down_1, sends_down_1)
+    send(bottom, top, halo_sem.at[4], down_1, sends_down_1)
+    send(bottom, top, halo_sem.at[4], down_1, jnp.logical_and(slab == 16, second))
+    send(own_low, to_2, halo_sem.at[3], down_2, sends_down_2)
+    send(own, from_1, halo_sem.at[0], up_1, sends_up_1)
+    send(own_high, from_2, halo_sem.at[2], up_2, sends_up_2)
+    cross(DOWNWARD)
     loads[3].wait()
     read_target(obs, target, src)
     one_hots(place_row, lane_row, row_hot, lane_hot)
 
     arrived(recv_xy.at[pl.ds(0, 15)], xy_sem)
     zsum[...] = lax.fori_loop(1, 16, lambda k, acc: acc + recv_xy[k], recv_xy[0], unroll=True)
-    wait_for(ready_z, 1 - zh)
+    wait_for(ready_halo, crossing)
+    cross(UPWARD)
+    wait_for(ready_z, number(first))
     send(zsum, recv_z, z_sem, z_peer)
-    wait_for(ready_halo, crossing)
-    send(*up_1, at_1)
-    send(*up_2, at_2)
-
-    @pl.when(slab > 0)
-    def _():
-        arrived(cext.at[pl.ds(2, DEPTH)], halo_sem.at[0])
-
-    @pl.when(slab > 1)
-    def _():
-        arrived(cext.at[pl.ds(0, 2)], halo_sem.at[2])
-
-    @pl.when(slab < 31)
-    def _():
-        arrived(cext.at[pl.ds(10, DEPTH)], halo_sem.at[1])
-        arrived(fext.at[pl.ds(DEPTH, 1)], halo_sem.at[4])
-
-    @pl.when(slab < 30)
-    def _():
-        arrived(cext.at[pl.ds(14, 2)], halo_sem.at[3])
+
+    held_field = jnp.logical_and(slab == 16, first)
+    wait_for(ready_field, number(held_field))
+    send(bottom, top, halo_sem.at[4], down_1, held_field)
+    wait_for(ready_core, core)
+    wait_for(ready_src, 7 - before)
+
+    for _, to, _, put, k in UPWARD + DOWNWARD:
+        block = cext.at[put + core]
+
+        @pl.when(slab == to)
+        def _():
+            arrived(block, cross_sem.at[k])
+
+        send(block, block, swap_sem.at[k], sibling, slab == to)
+        for step in range(1, 4):
+            z = jnp.where(zl == 0, step, 7 - step)
+            send(block, block, cross_sem.at[k], (z * 2 + core, slab), jnp.logical_and(edge, slab == to))
+    for _, to, _, put, k in UPWARD + DOWNWARD:
+
+        @pl.when(slab == to)
+        def _():
+            arrived(cext.at[put + 1 - core], swap_sem.at[k])
+
+    for buffer, arrival, when in (
+        (from_1, halo_sem.at[0], jnp.logical_not(among(0, 16))),
+        (to_1, halo_sem.at[1], jnp.logical_not(among(15, 31))),
+        (from_2, halo_sem.at[2], jnp.logical_not(among(0, 1, 16, 17))),
+        (to_2, halo_sem.at[3], jnp.logical_not(among(14, 15, 30, 31))),
+        (top, halo_sem.at[4], slab < 31),
+    ):
+
+        @pl.when(when)
+        def _():
+            arrived(buffer, arrival)
 
     conductivity_terms(cext, coef, diag, invd, cinv, slab)
     field_terms(fext, hu, slab)
-    wait_for(ready_core, core)
-    wait_for(ready_src, 7 - before)
-
     arrived(recv_z, z_sem)
     res = (zsum[...] + recv_z[...]) - target[...]
     for j in range(RROWS):
@@ -582,7 +634,7 @@
             pltpu.VMEM((8, 8, NX), F32),
             pltpu.VMEM((8, 8, NX), F32),
             dma((4,)), dma, dma((5,)), dma, dma, dma((2,)), dma, dma,
-            regular, regular, regular, regular,
+            dma((3,)), dma((3,)), regular, regular, regular, regular, regular,
         ],
         compiler_params=pltpu.CompilerParams(
             collective_id=0, has_side_effects=True, vmem_limit_bytes=32 * 1024 * 1024
@@ -594,6 +646,7 @@
         out_shape=(jax.ShapeDtypeStruct((8, NX), F32), jax.ShapeDtypeStruct((1, NX), F32)),
         in_specs=[vmem] * 2,
         out_specs=(vmem, vmem),
+        compiler_params=pltpu.CompilerParams(vmem_limit_bytes=1024 * 1024),
     )(*received)
     return grad.reshape(DEPTH, 2, NX), misfit[0, 0]
 

time: 47.1 us -> 43.8 us (0.930)
  the two profiles are of different devices: /device:TPU:1 before, /device:TPU:31 now
where the time goes in v4:
time: 43.8 us; the launch traced here: 43.6 us
  Pallas kernels  42.9 us (98%)
  between operations  0.64 us (1%)
    pallas_call x1, Pallas kernels, on_device(): pl.pallas_call(kernel, name='adjoint_gradient', out_shape=(jax.ShapeDtype...  42.3 us

profile of v4, /device:TPU:31, one launch (start us, length us, event | category | flops | bytes accessed | tf_op | source)
XLA Modules:
  0.0 43.6 jit_solution(6138123177811838928)
XLA Ops:
  0.6 42.3 %adjoint_gradient.1 = (f32[8,8,128]{2,1,0:T(8,128)S(1)}, f32[8,1,128]{2,1,0:T(1,128)S(1)}) custom-call(f32[4,32,128]{2,1,0:T(8,128)} %cond_hbm.1, f32[4,32,128]{2,1,0:T(8,128)} %bitcast.7, s32[2,2000]{1,0:T(2,128)} %bitcast.8, f32[16,2000]{1,0:T(8,128)} %obs_hbm.1), custom_call_target="tpu_custom_call" | custom-call | tf_op jit(solution)/shard_map/adjoint_gradient/pallas_call | solution.py:594
  43.0 0.6 %add_groups.1 = (f32[8,128]{1,0:T(8,128)}, f32[1,128]{1,0:T(1,128)}) custom-call(f32[8,8,128]{2,1,0:T(8,128)S(1)} %get-tuple-element.6.recv_src, f32[8,1,128]{2,1,0:T(1,128)S(1)} %get-tuple-element.7.recv_mis), custom_call_target="tpu_custom_call" | custom-call | tf_op jit(solution)/shard_map/add_groups/pallas_call | solution.py:643

commit v5 on v4

--- a/solution.py
+++ b/solution.py
@@ -212,7 +212,7 @@
     lax.fori_loop(1, 6, coarse, coarse_box(0), unroll=True)
 
 
-def field_terms(fext, hu, slab):
+def field_terms(fext, hu, slab, start, stop):
     def terms(p, low):
         high = forward(jnp.where(inside(p + 1, slab), fext[p + 1], 0.0))
         scales = (-ONE, -ONE, -TWO, -ONE, -TWO, -TWO, -THREE)
@@ -220,7 +220,7 @@
             hu[p, k] = term * scale
         return high
 
-    lax.fori_loop(0, DEPTH, terms, forward(fext[0]), unroll=True)
+    lax.fori_loop(start, stop, terms, forward(fext[start]), unroll=True)
 
 
 def spread_residual(res_row, lane_hot, lane_res):
@@ -333,12 +333,9 @@
     zl, core = src // 2, src % 2
     zh, px, py = slab // 16, (slab // 4) % 4, slab % 4
     here = px * 4 + py
-    plane_peers = [
-        (src, zh * 16 + ((px + i) % 4) * 4 + (py + j) % 4)
-        for i in range(4)
-        for j in range(4)
-        if i + j
-    ]
+    hops = (0, 1, 2, 1)
+    offsets = sorted(((i, j) for i in range(4) for j in range(4)), key=lambda o: -hops[o[0]] - hops[o[1]])
+    plane_peers = [(src, zh * 16 + ((px + i) % 4) * 4 + (py + j) % 4) for i, j in offsets[:-1]]
     z_peer = (src, (1 - zh) * 16 + here)
     sibling = (zl * 2 + 1 - core, slab)
     low_half, high_half = zh == 0, zh == 1
@@ -526,7 +523,6 @@
         (to_1, halo_sem.at[1], jnp.logical_not(among(15, 31))),
         (from_2, halo_sem.at[2], jnp.logical_not(among(0, 1, 16, 17))),
         (to_2, halo_sem.at[3], jnp.logical_not(among(14, 15, 30, 31))),
-        (top, halo_sem.at[4], slab < 31),
     ):
 
         @pl.when(when)
@@ -534,7 +530,7 @@
             arrived(buffer, arrival)
 
     conductivity_terms(cext, coef, diag, invd, cinv, slab)
-    field_terms(fext, hu, slab)
+    field_terms(fext, hu, slab, 0, DEPTH - 1)
     arrived(recv_z, z_sem)
     res = (zsum[...] + recv_z[...]) - target[...]
     for j in range(RROWS):
@@ -555,14 +551,19 @@
         send(mis_sum, recv_mis.at[zl], mis_sem.at[1], (z * 2 + core, slab))
 
     solve(coef, diag, invd, cinv, resid, direct, work, pe, lam)
+
+    @pl.when(slab < 31)
+    def _():
+        arrived(top, halo_sem.at[4])
+
+    field_terms(fext, hu, slab, DEPTH - 1, DEPTH)
     cell_products(lam, hu, chunks)
 
     send(chunks.at[1 - core], recv_core, core_sem, sibling)
     arrived(recv_core, core_sem)
     merged[...] = chunks[core] + recv_core[...]
-    for k in range(1, 8):
-        z = (zl + k) % 8
-        send(merged.at[z], recv_src.at[zl], src_sem, (z * 2 + core, slab))
+    for z in range(8):
+        send(merged.at[z], recv_src.at[zl], src_sem, (z * 2 + core, slab), zl != z)
     recv_src[zl] = merged[zl]
     arrived(recv_mis.at[pl.ds(0, 7)], mis_sem.at[1])
     arrived(recv_src.at[pl.ds(0, 7)], src_sem)

time: 43.8 us -> 39.5 us (0.902)
  the two profiles are of different devices: /device:TPU:31 before, /device:TPU:1 now
where the time goes in v5:
time: 39.5 us; the launch traced here: 39.3 us
  Pallas kernels  38.7 us (98%)
  between operations  0.64 us (2%)
    pallas_call x1, Pallas kernels, on_device(): pl.pallas_call(kernel, name='adjoint_gradient', out_shape=(jax.ShapeDtype...  38 us

profile of v5, /device:TPU:1, one launch (start us, length us, event | category | flops | bytes accessed | tf_op | source)
XLA Modules:
  0.0 39.3 jit_solution(13962619283946510750)
XLA Ops:
  0.6 38.0 %adjoint_gradient.1 = (f32[8,8,128]{2,1,0:T(8,128)S(1)}, f32[8,1,128]{2,1,0:T(1,128)S(1)}) custom-call(f32[4,32,128]{2,1,0:T(8,128)} %cond_hbm.1, f32[4,32,128]{2,1,0:T(8,128)} %bitcast.7, s32[2,2000]{1,0:T(2,128)} %bitcast.8, f32[16,2000]{1,0:T(8,128)} %obs_hbm.1), custom_call_target="tpu_custom_call" | custom-call | tf_op jit(solution)/shard_map/adjoint_gradient/pallas_call | solution.py:595
  38.7 0.6 %add_groups.1 = (f32[8,128]{1,0:T(8,128)}, f32[1,128]{1,0:T(1,128)}) custom-call(f32[8,8,128]{2,1,0:T(8,128)S(1)} %get-tuple-element.6.recv_src, f32[8,1,128]{2,1,0:T(1,128)S(1)} %get-tuple-element.7.recv_mis), custom_call_target="tpu_custom_call" | custom-call | tf_op jit(solution)/shard_map/add_groups/pallas_call | solution.py:644

commit v6 on v5

--- a/solution.py
+++ b/solution.py
@@ -21,7 +21,6 @@
 NY, NX = 32, 128
 DEPTH = 4
 BELOW = 5
-BLOCK = 15
 PLANES = 15
 CELLS = 16
 RX = 2000
@@ -223,32 +222,22 @@
     lax.fori_loop(start, stop, terms, forward(fext[start]), unroll=True)
 
 
-def spread_residual(res_row, lane_hot, lane_res):
-    def spread(j, carry):
-        columns = pl.ds(pl.multiple_of(j * NX, NX), NX)
+def scatter(res_row, row_hot, lane_hot, invd, resid):
+    high_parts, low_parts = [], []
+    for j in range(IDX):
         value = jnp.broadcast_to(res_row[j], (16, NX))
         high = value.astype(jnp.bfloat16)
         low = (value - high.astype(F32)).astype(jnp.bfloat16)
-        hot = lane_hot[:, columns].reshape(NX // 16, 16, NX)
-        lane_res[0:NX, columns] = (hot * high[None]).reshape(NX, NX)
-        lane_res[NX:, columns] = (hot * low[None]).reshape(NX, NX)
-        return carry
-
-    lax.fori_loop(0, IDX, spread, 0, unroll=4)
-
-
-def scatter(row_hot, lane_res, invd, resid):
-    def product(q, carry):
-        span = pl.ds(pl.multiple_of(q * (BLOCK * NY), BLOCK * NY), BLOCK * NY)
-        both = lax.dot_general(
-            row_hot[span, :], lane_res[...], (((1,), (1,)), ((), ())), preferred_element_type=F32
-        )
-        rhs = (both[:, :NX] + both[:, NX:]).reshape(BLOCK, NY, NX)
-        planes = pl.ds(q * BLOCK, BLOCK)
-        resid[planes] = rhs * invd[planes]
-        return carry
-
-    lax.fori_loop(0, PLANES // BLOCK, product, 0)
+        hot = lane_hot[:, j * NX : (j + 1) * NX].reshape(NX // 16, 16, NX)
+        high_parts.append((hot * high[None]).reshape(NX, NX))
+        low_parts.append((hot * low[None]).reshape(NX, NX))
+    by_lane = jnp.concatenate(
+        [jnp.concatenate(high_parts, axis=1), jnp.concatenate(low_parts, axis=1)], axis=0
+    )
+    both = lax.dot_general(
+        row_hot[...], by_lane, (((1,), (1,)), ((), ())), preferred_element_type=F32
+    )
+    resid[...] = (both[:, :NX] + both[:, NX:]).reshape(PLANES, NY, NX) * invd[...]
 
 
 def solve(coef, diag, invd, cinv, resid, direct, work, pe, lam):
@@ -322,11 +311,11 @@
     recv_src, recv_mis,
     cext, fext, pairs, obs, index, target,
     part, recv_xy, zsum, recv_z,
-    place_row, lane_row, res_row, row_hot, lane_hot, lane_res, coef, diag, invd, cinv, hu,
+    place_row, lane_row, res_row, row_hot, lane_hot, coef, diag, invd, cinv, hu,
     resid, direct, work, lam, pe,
     mis, mis_core, mis_sum, chunks, recv_core, merged,
     in_sem, send_sem, halo_sem, xy_sem, z_sem, mis_sem, core_sem, src_sem,
-    cross_sem, swap_sem, ready_z, ready_halo, ready_core, ready_src, ready_field,
+    cross_sem, swap_sem, go, ready,
 ):
     src = lax.axis_index("src")
     slab = lax.axis_index("slab")
@@ -338,14 +327,8 @@
     plane_peers = [(src, zh * 16 + ((px + i) % 4) * 4 + (py + j) % 4) for i, j in offsets[:-1]]
     z_peer = (src, (1 - zh) * 16 + here)
     sibling = (zl * 2 + 1 - core, slab)
-    low_half, high_half = zh == 0, zh == 1
-    first = jnp.where(zl < 4, zh, 1 - zh) == 0
-    second = jnp.logical_not(first)
     edge = jnp.logical_or(zl == 0, zl == 7)
     beyond = (7 - zl) * 2 + core
-    greets_field = jnp.logical_and(first, jnp.logical_or(slab == 15, slab == 16))
-    hears_field = jnp.logical_and(second, jnp.logical_or(slab == 15, slab == 16))
-    across = (src, 31 - slab)
 
     loads = [
         pltpu.make_async_copy(pairs_hbm, pairs, in_sem.at[0]),
@@ -361,33 +344,26 @@
     def signal(sem, peer):
         pl.semaphore_signal(sem, inc=1, device_id=peer, device_id_type=MESH)
 
-    for peer in plane_peers:
-        signal(barrier, peer)
-
-    @pl.when(first)
-    def _():
-        signal(barrier, z_peer)
-
-    for at, to in CROSSING:
-
-        @pl.when(jnp.logical_and(edge, slab == at))
-        def _():
-            signal(barrier, (beyond, to))
-
-    @pl.when(greets_field)
-    def _():
-        signal(barrier, across)
-
-    for z in range(8):
-        after = jnp.where(low_half, z > zl, z < zl)
-
-        @pl.when(after)
-        def _():
-            signal(barrier, (z * 2 + core, slab))
+    for _, peer in plane_peers:
+        signal(barrier, (zl * 2, peer))
 
     @pl.when(core == 1)
     def _():
         signal(barrier, sibling)
+
+    signal(barrier, (zl * 2 + 1, (1 - zh) * 16 + here))
+    for k in range(1, 8):
+        signal(barrier, (((zl + k) % 8) * 2 + 1, slab))
+    for low, high in CROSSING:
+        for at, to in ((low, high), (high, low)):
+
+            @pl.when(jnp.logical_and(edge, slab == at))
+            def _():
+                signal(barrier, ((7 - zl) * 2 + 1, to))
+
+    @pl.when(slab == 15)
+    def _():
+        signal(barrier, (zl * 2 + 1, 16))
 
     loads[0].wait()
     read_pairs(pairs, index, place_row, lane_row, slab)
@@ -411,48 +387,20 @@
     def arrived(buffer, arrival):
         pltpu.make_async_copy(buffer, buffer, arrival).wait()
 
-    def wait_for(sem, count):
-        @pl.when(count > 0)
-        def _():
-            pl.semaphore_wait(sem, count)
-
-    def number(flag):
-        return flag.astype(jnp.int32)
-
-    crossed = sum(number(slab == to) for _, to in CROSSING) * number(edge)
-    crossing = sum(number(slab == at) for at, _ in CROSSING) * number(edge)
-    before = jnp.where(low_half, zl, 7 - zl)
-    heard = 15 + number(second) + crossed + number(hears_field) + before + (1 - core)
-    pl.semaphore_wait(barrier, heard)
+    @pl.when(core == 0)
+    def _():
+        pl.semaphore_wait(barrier, 2 * 15 + 1)
+        signal(go, sibling)
+
+    @pl.when(core == 1)
+    def _():
+        pl.semaphore_wait(go, 1)
+
     for peer in plane_peers:
         send(part, recv_xy.at[here], xy_sem, peer)
 
-    @pl.when(second)
-    def _():
-        signal(ready_z, z_peer)
-
-    for at, to in CROSSING:
-
-        @pl.when(jnp.logical_and(edge, slab == to))
-        def _():
-            signal(ready_halo, (beyond, at))
-
-    @pl.when(jnp.logical_and(hears_field, slab == 15))
-    def _():
-        signal(ready_field, across)
-
-    for z in range(8):
-        earlier = jnp.where(low_half, z < zl, z > zl)
-
-        @pl.when(earlier)
-        def _():
-            signal(ready_src, (z * 2 + core, slab))
-
-    @pl.when(core == 0)
-    def _():
-        signal(ready_core, sibling)
-
     loads[2].wait()
+
     def cross(blocks):
         for at, to, take, put, k in blocks:
             send(
@@ -479,27 +427,31 @@
     bottom = fext.at[pl.ds(0, 1)]
     send(own, to_1, halo_sem.at[1], down_1, sends_down_1)
     send(bottom, top, halo_sem.at[4], down_1, sends_down_1)
-    send(bottom, top, halo_sem.at[4], down_1, jnp.logical_and(slab == 16, second))
     send(own_low, to_2, halo_sem.at[3], down_2, sends_down_2)
     send(own, from_1, halo_sem.at[0], up_1, sends_up_1)
     send(own_high, from_2, halo_sem.at[2], up_2, sends_up_2)
-    cross(DOWNWARD)
+
+    crossed = sum((slab == t).astype(jnp.int32) for pair in CROSSING for t in pair)
+    far = 1 + 7 + crossed * edge.astype(jnp.int32) + (slab == 16).astype(jnp.int32)
+
+    @pl.when(core == 1)
+    def _():
+        pl.semaphore_wait(barrier, 2 * far)
+        signal(ready, sibling)
+
+    @pl.when(core == 0)
+    def _():
+        pl.semaphore_wait(ready, 1)
+
+    cross(DOWNWARD + UPWARD)
+    send(bottom, top, halo_sem.at[4], down_1, slab == 16)
     loads[3].wait()
     read_target(obs, target, src)
     one_hots(place_row, lane_row, row_hot, lane_hot)
 
     arrived(recv_xy.at[pl.ds(0, 15)], xy_sem)
     zsum[...] = lax.fori_loop(1, 16, lambda k, acc: acc + recv_xy[k], recv_xy[0], unroll=True)
-    wait_for(ready_halo, crossing)
-    cross(UPWARD)
-    wait_for(ready_z, number(first))
     send(zsum, recv_z, z_sem, z_peer)
-
-    held_field = jnp.logical_and(slab == 16, first)
-    wait_for(ready_field, number(held_field))
-    send(bottom, top, halo_sem.at[4], down_1, held_field)
-    wait_for(ready_core, core)
-    wait_for(ready_src, 7 - before)
 
     for _, to, _, put, k in UPWARD + DOWNWARD:
         block = cext.at[put + core]
@@ -540,8 +492,7 @@
     mis[...] = jnp.broadcast_to(half, (1, NX))
     send(mis, mis_core, mis_sem.at[0], sibling)
 
-    spread_residual(res_row, lane_hot, lane_res)
-    scatter(row_hot, lane_res, invd, resid)
+    scatter(res_row, row_hot, lane_hot, invd, resid)
 
     arrived(mis_core, mis_sem.at[0])
     mis_sum[...] = mis[...] + mis_core[...]
@@ -617,7 +568,6 @@
             pltpu.VMEM((IDX, 1, NX), F32),
             pltpu.VMEM((PLANES * NY, IDX * NX), jnp.bfloat16),
             pltpu.VMEM((NX, IDX * NX), jnp.bfloat16),
-            pltpu.VMEM((2 * NX, IDX * NX), jnp.bfloat16),
             pltpu.VMEM((3, PLANES, *plane), F32),
             pltpu.VMEM((PLANES, *plane), F32),
             pltpu.VMEM((PLANES, *plane), F32),
@@ -635,7 +585,7 @@
             pltpu.VMEM((8, 8, NX), F32),
             pltpu.VMEM((8, 8, NX), F32),
             dma((4,)), dma, dma((5,)), dma, dma, dma((2,)), dma, dma,
-            dma((3,)), dma((3,)), regular, regular, regular, regular, regular,
+            dma((3,)), dma((3,)), regular, regular,
         ],
         compiler_params=pltpu.CompilerParams(
             collective_id=0, has_side_effects=True, vmem_limit_bytes=32 * 1024 * 1024

time: 39.5 us -> 39.1 us (0.990)
  Pallas kernels: 38.7 us -> 38.2 us
    pallas_call x1, Pallas kernels: 38 us -> 37.6 us  [on_device(): pl.pallas_call(kernel, name='adjoint_gradient', out_shape=(jax.ShapeDtype...]
where the time goes in v6:
time: 39.1 us; the launch traced here: 38.9 us
  Pallas kernels  38.2 us (98%)
  between operations  0.64 us (2%)
    pallas_call x1, Pallas kernels, on_device(): pl.pallas_call(kernel, name='adjoint_gradient', out_shape=(jax.ShapeDtype...  37.6 us

profile of v6, /device:TPU:1, one launch (start us, length us, event | category | flops | bytes accessed | tf_op | source)
XLA Modules:
  0.0 38.9 jit_solution(2354539200458563475)
XLA Ops:
  0.6 37.6 %adjoint_gradient.1 = (f32[8,8,128]{2,1,0:T(8,128)S(1)}, f32[8,1,128]{2,1,0:T(1,128)S(1)}) custom-call(f32[4,32,128]{2,1,0:T(8,128)} %cond_hbm.1, f32[4,32,128]{2,1,0:T(8,128)} %bitcast.7, s32[2,2000]{1,0:T(2,128)} %bitcast.8, f32[16,2000]{1,0:T(8,128)} %obs_hbm.1), custom_call_target="tpu_custom_call" | custom-call | tf_op jit(solution)/shard_map/adjoint_gradient/pallas_call | solution.py:546
  38.3 0.6 %add_groups.1 = (f32[8,128]{1,0:T(8,128)}, f32[1,128]{1,0:T(1,128)}) custom-call(f32[8,8,128]{2,1,0:T(8,128)S(1)} %get-tuple-element.6.recv_src, f32[8,1,128]{2,1,0:T(1,128)S(1)} %get-tuple-element.7.recv_mis), custom_call_target="tpu_custom_call" | custom-call | tf_op jit(solution)/shard_map/add_groups/pallas_call | solution.py:594

commit v7 on v6

--- a/solution.py
+++ b/solution.py
@@ -314,7 +314,7 @@
     place_row, lane_row, res_row, row_hot, lane_hot, coef, diag, invd, cinv, hu,
     resid, direct, work, lam, pe,
     mis, mis_core, mis_sum, chunks, recv_core, merged,
-    in_sem, send_sem, halo_sem, xy_sem, z_sem, mis_sem, core_sem, src_sem,
+    in_sem, send_sem, sum_sem, halo_sem, xy_sem, z_sem, mis_sem, core_sem, src_sem,
     cross_sem, swap_sem, go, ready,
 ):
     src = lax.axis_index("src")
@@ -325,7 +325,6 @@
     hops = (0, 1, 2, 1)
     offsets = sorted(((i, j) for i in range(4) for j in range(4)), key=lambda o: -hops[o[0]] - hops[o[1]])
     plane_peers = [(src, zh * 16 + ((px + i) % 4) * 4 + (py + j) % 4) for i, j in offsets[:-1]]
-    z_peer = (src, (1 - zh) * 16 + here)
     sibling = (zl * 2 + 1 - core, slab)
     edge = jnp.logical_or(zl == 0, zl == 7)
     beyond = (7 - zl) * 2 + core
@@ -344,32 +343,35 @@
     def signal(sem, peer):
         pl.semaphore_signal(sem, inc=1, device_id=peer, device_id_type=MESH)
 
-    for _, peer in plane_peers:
-        signal(barrier, (zl * 2, peer))
-
-    @pl.when(core == 1)
+    for peer in plane_peers:
+        signal(barrier, peer)
+
+    @pl.when(core == 0)
     def _():
         signal(barrier, sibling)
 
-    signal(barrier, (zl * 2 + 1, (1 - zh) * 16 + here))
+    signal(barrier, (zl * 2, (1 - zh) * 16 + here))
     for k in range(1, 8):
-        signal(barrier, (((zl + k) % 8) * 2 + 1, slab))
+        signal(barrier, (((zl + k) % 8) * 2, slab))
     for low, high in CROSSING:
         for at, to in ((low, high), (high, low)):
 
             @pl.when(jnp.logical_and(edge, slab == at))
             def _():
-                signal(barrier, ((7 - zl) * 2 + 1, to))
+                signal(barrier, ((7 - zl) * 2, to))
 
     @pl.when(slab == 15)
     def _():
-        signal(barrier, (zl * 2 + 1, 16))
+        signal(barrier, (zl * 2, 16))
 
     loads[0].wait()
     read_pairs(pairs, index, place_row, lane_row, slab)
     loads[1].wait()
     gather(fext, index, part, slab)
-    recv_xy[here] = part[...]
+
+    @pl.when(core == 1)
+    def _():
+        recv_xy[1, here] = part[...]
 
     sent = []
 
@@ -387,17 +389,30 @@
     def arrived(buffer, arrival):
         pltpu.make_async_copy(buffer, buffer, arrival).wait()
 
+    @pl.when(core == 1)
+    def _():
+        pl.semaphore_wait(barrier, 15 + 1)
+        signal(go, sibling)
+
     @pl.when(core == 0)
     def _():
-        pl.semaphore_wait(barrier, 2 * 15 + 1)
-        signal(go, sibling)
+        pl.semaphore_wait(go, 1)
+
+    for _, peer in plane_peers:
+        send(part, recv_xy.at[core, here], xy_sem.at[core], (zl * 2 + 1, peer))
+    send(part, recv_xy.at[0, here], xy_sem.at[0], sibling, core == 0)
+
+    crossed = sum((slab == t).astype(jnp.int32) for pair in CROSSING for t in pair)
+    far = 1 + 7 + crossed * edge.astype(jnp.int32) + (slab == 16).astype(jnp.int32)
+
+    @pl.when(core == 0)
+    def _():
+        pl.semaphore_wait(barrier, 15 + 2 * far)
+        signal(ready, sibling)
 
     @pl.when(core == 1)
     def _():
-        pl.semaphore_wait(go, 1)
-
-    for peer in plane_peers:
-        send(part, recv_xy.at[here], xy_sem, peer)
+        pl.semaphore_wait(ready, 1)
 
     loads[2].wait()
 
@@ -431,27 +446,38 @@
     send(own, from_1, halo_sem.at[0], up_1, sends_up_1)
     send(own_high, from_2, halo_sem.at[2], up_2, sends_up_2)
 
-    crossed = sum((slab == t).astype(jnp.int32) for pair in CROSSING for t in pair)
-    far = 1 + 7 + crossed * edge.astype(jnp.int32) + (slab == 16).astype(jnp.int32)
-
-    @pl.when(core == 1)
-    def _():
-        pl.semaphore_wait(barrier, 2 * far)
-        signal(ready, sibling)
-
-    @pl.when(core == 0)
-    def _():
-        pl.semaphore_wait(ready, 1)
-
     cross(DOWNWARD + UPWARD)
-    send(bottom, top, halo_sem.at[4], down_1, slab == 16)
     loads[3].wait()
     read_target(obs, target, src)
     one_hots(place_row, lane_row, row_hot, lane_hot)
 
-    arrived(recv_xy.at[pl.ds(0, 15)], xy_sem)
-    zsum[...] = lax.fori_loop(1, 16, lambda k, acc: acc + recv_xy[k], recv_xy[0], unroll=True)
-    send(zsum, recv_z, z_sem, z_peer)
+    def add_plane(k):
+        return lax.fori_loop(1, 16, lambda i, acc: acc + recv_xy[k, i], recv_xy[k, 0], unroll=True)
+
+    def send_sum(source, to, slot):
+        return pltpu.make_async_remote_copy(
+            src_ref=source, dst_ref=to[0], send_sem=sum_sem.at[slot], recv_sem=to[1],
+            device_id=to[2], device_id_type=MESH,
+        )
+
+    other_half = (1 - zh) * 16 + here
+    sums = [
+        send_sum(zsum.at[1], (recv_z, z_sem.at[1], (zl * 2, other_half)), 0),
+        send_sum(zsum.at[1], (zsum.at[0], z_sem.at[0], sibling), 1),
+        send_sum(zsum.at[0], (recv_z, z_sem.at[1], (zl * 2 + 1, other_half)), 2),
+    ]
+
+    @pl.when(core == 1)
+    def _():
+        arrived(recv_xy.at[0], xy_sem.at[0])
+        zsum[1] = add_plane(0)
+        sums[0].start()
+        sums[1].start()
+        arrived(recv_xy.at[1, pl.ds(0, 15)], xy_sem.at[1])
+        zsum[0] = add_plane(1)
+        sums[2].start()
+
+    send(bottom, top, halo_sem.at[4], down_1, slab == 16)
 
     for _, to, _, put, k in UPWARD + DOWNWARD:
         block = cext.at[put + core]
@@ -483,8 +509,13 @@
 
     conductivity_terms(cext, coef, diag, invd, cinv, slab)
     field_terms(fext, hu, slab, 0, DEPTH - 1)
-    arrived(recv_z, z_sem)
-    res = (zsum[...] + recv_z[...]) - target[...]
+
+    @pl.when(core == 0)
+    def _():
+        arrived(zsum.at[0], z_sem.at[0])
+
+    arrived(recv_z, z_sem.at[1])
+    res = (zsum[0] + recv_z[...]) - target[...]
     for j in range(RROWS):
         res_row[j] = res[j : j + 1, :]
         res_row[RROWS + j] = -res[j : j + 1, :]
@@ -518,6 +549,12 @@
     recv_src[zl] = merged[zl]
     arrived(recv_mis.at[pl.ds(0, 7)], mis_sem.at[1])
     arrived(recv_src.at[pl.ds(0, 7)], src_sem)
+
+    @pl.when(core == 1)
+    def _():
+        for copy in sums:
+            copy.wait_send()
+
     for wait, when in sent:
         if when is None:
             wait()
@@ -560,8 +597,8 @@
             pltpu.VMEM((IDX, NX), jnp.int32),
             pltpu.VMEM((RROWS, NX), F32),
             pltpu.VMEM((RROWS, NX), F32),
-            pltpu.VMEM((16, RROWS, NX), F32),
-            pltpu.VMEM((RROWS, NX), F32),
+            pltpu.VMEM((2, 16, RROWS, NX), F32),
+            pltpu.VMEM((2, RROWS, NX), F32),
             pltpu.VMEM((RROWS, NX), F32),
             pltpu.VMEM((IDX, 1, NX), F32),
             pltpu.VMEM((IDX, 1, NX), F32),
@@ -584,7 +621,7 @@
             pltpu.VMEM((2, 8, 8, NX), F32),
             pltpu.VMEM((8, 8, NX), F32),
             pltpu.VMEM((8, 8, NX), F32),
-            dma((4,)), dma, dma((5,)), dma, dma, dma((2,)), dma, dma,
+            dma((4,)), dma, dma((3,)), dma((5,)), dma((2,)), dma((2,)), dma((2,)), dma, dma,
             dma((3,)), dma((3,)), regular, regular,
         ],
         compiler_params=pltpu.CompilerParams(

time: 39.1 us -> 38.8 us (level)
  no operation moved by 1% of the time
where the time goes in v7:
time: 38.8 us; the launch traced here: 38.6 us
  Pallas kernels  38 us (98%)
  between operations  0.64 us (2%)
    pallas_call x1, Pallas kernels, on_device(): pl.pallas_call(kernel, name='adjoint_gradient', out_shape=(jax.ShapeDtype...  37.4 us

profile of v7, /device:TPU:1, one launch (start us, length us, event | category | flops | bytes accessed | tf_op | source)
XLA Modules:
  0.0 38.6 jit_solution(13067523563848757166)
XLA Ops:
  0.6 37.4 %adjoint_gradient.1 = (f32[8,8,128]{2,1,0:T(8,128)S(1)}, f32[8,1,128]{2,1,0:T(1,128)S(1)}) custom-call(f32[4,32,128]{2,1,0:T(8,128)} %cond_hbm.1, f32[4,32,128]{2,1,0:T(8,128)} %bitcast.7, s32[2,2000]{1,0:T(2,128)} %bitcast.8, f32[16,2000]{1,0:T(8,128)} %obs_hbm.1), custom_call_target="tpu_custom_call" | custom-call | tf_op jit(solution)/shard_map/adjoint_gradient/pallas_call | solution.py:583
  38.0 0.6 %add_groups.1 = (f32[8,128]{1,0:T(8,128)}, f32[1,128]{1,0:T(1,128)}) custom-call(f32[8,8,128]{2,1,0:T(8,128)S(1)} %get-tuple-element.6.recv_src, f32[8,1,128]{2,1,0:T(1,128)S(1)} %get-tuple-element.7.recv_mis), custom_call_target="tpu_custom_call" | custom-call | tf_op jit(solution)/shard_map/add_groups/pallas_call | solution.py:631

commit v8 on v7

--- a/solution.py
+++ b/solution.py
@@ -254,15 +254,15 @@
     def second_step(p, applied):
         r2 = resid[p] - applied * invd[p]
         resid[p] = r2
-        f = diag[p] * r2
-        f = f + 0.5 * (prev_x(f) + next_x(f))
-        work[p] = f + 0.5 * (prev_y(f) + next_y(f))
+        work[p] = diag[p] * r2
 
     apply_planes(direct, coef, 2, 12, second_step)
 
     def correct(j):
         p = 2 * j + 3
-        c = (work[p] + 0.5 * (work[p - 1] + work[p + 1])) * cinv[j]
+        c = work[p] + 0.5 * (work[p - 1] + work[p + 1])
+        c = c + 0.5 * (prev_y(c) + next_y(c))
+        c = (c + 0.5 * (prev_x(c) + next_x(c))) * cinv[j]
         c = c + 0.5 * (prev_y(c) + next_y(c))
         return c + 0.5 * (prev_x(c) + next_x(c))
 
@@ -313,8 +313,8 @@
     part, recv_xy, zsum, recv_z,
     place_row, lane_row, res_row, row_hot, lane_hot, coef, diag, invd, cinv, hu,
     resid, direct, work, lam, pe,
-    mis, mis_core, mis_sum, chunks, recv_core, merged,
-    in_sem, send_sem, sum_sem, halo_sem, xy_sem, z_sem, mis_sem, core_sem, src_sem,
+    mis, chunks,
+    in_sem, send_sem, sum_sem, halo_sem, xy_sem, z_sem, mis_sem, src_sem,
     cross_sem, swap_sem, go, ready,
 ):
     src = lax.axis_index("src")
@@ -519,18 +519,14 @@
     for j in range(RROWS):
         res_row[j] = res[j : j + 1, :]
         res_row[RROWS + j] = -res[j : j + 1, :]
+    scatter(res_row, row_hot, lane_hot, invd, resid)
+
     half = jnp.sum(jnp.sum(0.5 * res * res, axis=0, keepdims=True), axis=1, keepdims=True)
     mis[...] = jnp.broadcast_to(half, (1, NX))
-    send(mis, mis_core, mis_sem.at[0], sibling)
-
-    scatter(res_row, row_hot, lane_hot, invd, resid)
-
-    arrived(mis_core, mis_sem.at[0])
-    mis_sum[...] = mis[...] + mis_core[...]
-    recv_mis[zl] = mis_sum[...]
-    for k in range(1, 8):
-        z = (zl + k) % 8
-        send(mis_sum, recv_mis.at[zl], mis_sem.at[1], (z * 2 + core, slab))
+    recv_mis[src] = mis[...]
+    for z in range(8):
+        for c in (1, 0):
+            send(mis, recv_mis.at[src], mis_sem, (z * 2 + c, slab), src != z * 2 + c)
 
     solve(coef, diag, invd, cinv, resid, direct, work, pe, lam)
 
@@ -541,14 +537,12 @@
     field_terms(fext, hu, slab, DEPTH - 1, DEPTH)
     cell_products(lam, hu, chunks)
 
-    send(chunks.at[1 - core], recv_core, core_sem, sibling)
-    arrived(recv_core, core_sem)
-    merged[...] = chunks[core] + recv_core[...]
     for z in range(8):
-        send(merged.at[z], recv_src.at[zl], src_sem, (z * 2 + core, slab), zl != z)
-    recv_src[zl] = merged[zl]
-    arrived(recv_mis.at[pl.ds(0, 7)], mis_sem.at[1])
-    arrived(recv_src.at[pl.ds(0, 7)], src_sem)
+        for c in (1, 0):
+            send(chunks.at[c, z], recv_src.at[src], src_sem, (z * 2 + c, slab), src != z * 2 + c)
+    recv_src[src] = chunks[core, zl]
+    arrived(recv_mis.at[pl.ds(0, 15)], mis_sem)
+    arrived(recv_src.at[pl.ds(0, 15)], src_sem)
 
     @pl.when(core == 1)
     def _():
@@ -564,7 +558,7 @@
 
 def finish(recv_src, recv_mis, grad_ref, misfit_ref):
     total, misfit = recv_src[0], recv_mis[0]
-    for k in range(1, 8):
+    for k in range(1, GROUPS):
         total, misfit = total + recv_src[k], misfit + recv_mis[k]
     grad_ref[...] = total
     misfit_ref[...] = misfit * (1.0 / (GROUPS * RX))
@@ -584,8 +578,8 @@
         kernel,
         name="adjoint_gradient",
         out_shape=(
-            jax.ShapeDtypeStruct((8, 8, NX), F32),
-            jax.ShapeDtypeStruct((8, 1, NX), F32),
+            jax.ShapeDtypeStruct((GROUPS, 8, NX), F32),
+            jax.ShapeDtypeStruct((GROUPS, 1, NX), F32),
         ),
         in_specs=[any_spec] * 4,
         out_specs=(vmem, vmem),
@@ -616,12 +610,8 @@
             pltpu.VMEM((PLANES, *plane), F32),
             pltpu.VMEM((PLANES, *plane), F32),
             pltpu.VMEM((1, NX), F32),
-            pltpu.VMEM((1, NX), F32),
-            pltpu.VMEM((1, NX), F32),
             pltpu.VMEM((2, 8, 8, NX), F32),
-            pltpu.VMEM((8, 8, NX), F32),
-            pltpu.VMEM((8, 8, NX), F32),
-            dma((4,)), dma, dma((3,)), dma((5,)), dma((2,)), dma((2,)), dma((2,)), dma, dma,
+            dma((4,)), dma, dma((3,)), dma((5,)), dma((2,)), dma((2,)), dma, dma,
             dma((3,)), dma((3,)), regular, regular,
         ],
         compiler_params=pltpu.CompilerParams(

time: 38.8 us -> 38.3 us (0.987)
  Pallas kernels: 38 us -> 37.4 us
    pallas_call x1, Pallas kernels: 37.4 us -> 36.8 us  [on_device(): pl.pallas_call(kernel, name='adjoint_gradient', out_shape=(jax.ShapeDtype...]
where the time goes in v8:
time: 38.3 us; the launch traced here: 38.1 us
  Pallas kernels  37.4 us (98%)
  between operations  0.64 us (2%)
    pallas_call x1, Pallas kernels, on_device(): pl.pallas_call(kernel, name='adjoint_gradient', out_shape=(jax.ShapeDtype...  36.8 us

profile of v8, /device:TPU:1, one launch (start us, length us, event | category | flops | bytes accessed | tf_op | source)
XLA Modules:
  0.0 38.1 jit_solution(8681516002396370785)
XLA Ops:
  0.6 36.8 %adjoint_gradient.1 = (f32[16,8,128]{2,1,0:T(8,128)S(1)}, f32[16,1,128]{2,1,0:T(1,128)S(1)}) custom-call(f32[4,32,128]{2,1,0:T(8,128)} %cond_hbm.1, f32[4,32,128]{2,1,0:T(8,128)} %bitcast.7, s32[2,2000]{1,0:T(2,128)} %bitcast.8, f32[16,2000]{1,0:T(8,128)} %obs_hbm.1), custom_call_target="tpu_custom_call" | custom-call | tf_op jit(solution)/shard_map/adjoint_gradient/pallas_call | solution.py:577
  37.5 0.6 %add_groups.1 = (f32[8,128]{1,0:T(8,128)}, f32[1,128]{1,0:T(1,128)}) custom-call(f32[16,8,128]{2,1,0:T(8,128)S(1)} %get-tuple-element.6.recv_src, f32[16,1,128]{2,1,0:T(1,128)S(1)} %get-tuple-element.7.recv_mis), custom_call_target="tpu_custom_call" | custom-call | tf_op jit(solution)/shard_map/add_groups/pallas_call | solution.py:621

commit v9 on v8

--- a/solution.py
+++ b/solution.py
@@ -440,16 +440,19 @@
     sends_down_1, sends_down_2 = (jnp.logical_not(among(*t)) for t in ((0, 16), (0, 1, 16, 17)))
     top = fext.at[pl.ds(DEPTH, 1)]
     bottom = fext.at[pl.ds(0, 1)]
+    cross(DOWNWARD + UPWARD)
     send(own, to_1, halo_sem.at[1], down_1, sends_down_1)
     send(bottom, top, halo_sem.at[4], down_1, sends_down_1)
     send(own_low, to_2, halo_sem.at[3], down_2, sends_down_2)
     send(own, from_1, halo_sem.at[0], up_1, sends_up_1)
     send(own_high, from_2, halo_sem.at[2], up_2, sends_up_2)
 
-    cross(DOWNWARD + UPWARD)
     loads[3].wait()
     read_target(obs, target, src)
-    one_hots(place_row, lane_row, row_hot, lane_hot)
+
+    @pl.when(among(14, 15))
+    def _():
+        one_hots(place_row, lane_row, row_hot, lane_hot)
 
     def add_plane(k):
         return lax.fori_loop(1, 16, lambda i, acc: acc + recv_xy[k, i], recv_xy[k, 0], unroll=True)
@@ -480,21 +483,28 @@
     send(bottom, top, halo_sem.at[4], down_1, slab == 16)
 
     for _, to, _, put, k in UPWARD + DOWNWARD:
-        block = cext.at[put + core]
 
         @pl.when(slab == to)
         def _():
-            arrived(block, cross_sem.at[k])
-
+            arrived(cext.at[put + core], cross_sem.at[k])
+
+    for _, to, _, put, k in UPWARD + DOWNWARD:
+        block = cext.at[put + core]
         send(block, block, swap_sem.at[k], sibling, slab == to)
-        for step in range(1, 4):
-            z = jnp.where(zl == 0, step, 7 - step)
+    for step in (3, 2, 1):
+        z = jnp.where(zl == 0, step, 7 - step)
+        for _, to, _, put, k in UPWARD + DOWNWARD:
+            block = cext.at[put + core]
             send(block, block, cross_sem.at[k], (z * 2 + core, slab), jnp.logical_and(edge, slab == to))
     for _, to, _, put, k in UPWARD + DOWNWARD:
 
         @pl.when(slab == to)
         def _():
             arrived(cext.at[put + 1 - core], swap_sem.at[k])
+
+    @pl.when(jnp.logical_not(among(14, 15)))
+    def _():
+        one_hots(place_row, lane_row, row_hot, lane_hot)
 
     for buffer, arrival, when in (
         (from_1, halo_sem.at[0], jnp.logical_not(among(0, 16))),

time: 38.3 us -> 36.7 us (0.958)
  Pallas kernels: 37.4 us -> 35.8 us
    pallas_call x1, Pallas kernels: 36.8 us -> 35.2 us  [on_device(): pl.pallas_call(kernel, name='adjoint_gradient', out_shape=(jax.ShapeDtype...]
where the time goes in v9:
time: 36.7 us; the launch traced here: 36.4 us
  Pallas kernels  35.8 us (98%)
  between operations  0.64 us (2%)
    pallas_call x1, Pallas kernels, on_device(): pl.pallas_call(kernel, name='adjoint_gradient', out_shape=(jax.ShapeDtype...  35.2 us

profile of v9, /device:TPU:1, one launch (start us, length us, event | category | flops | bytes accessed | tf_op | source)
XLA Modules:
  0.0 36.4 jit_solution(6359600540399207328)
XLA Ops:
  0.6 35.2 %adjoint_gradient.1 = (f32[16,8,128]{2,1,0:T(8,128)S(1)}, f32[16,1,128]{2,1,0:T(1,128)S(1)}) custom-call(f32[4,32,128]{2,1,0:T(8,128)} %cond_hbm.1, f32[4,32,128]{2,1,0:T(8,128)} %bitcast.7, s32[2,2000]{1,0:T(2,128)} %bitcast.8, f32[16,2000]{1,0:T(8,128)} %obs_hbm.1), custom_call_target="tpu_custom_call" | custom-call | tf_op jit(solution)/shard_map/adjoint_gradient/pallas_call | solution.py:587
  35.8 0.6 %add_groups.1 = (f32[8,128]{1,0:T(8,128)}, f32[1,128]{1,0:T(1,128)}) custom-call(f32[16,8,128]{2,1,0:T(8,128)S(1)} %get-tuple-element.6.recv_src, f32[16,1,128]{2,1,0:T(1,128)S(1)} %get-tuple-element.7.recv_mis), custom_call_target="tpu_custom_call" | custom-call | tf_op jit(solution)/shard_map/add_groups/pallas_call | solution.py:631

commit v10 on v9

--- a/solution.py
+++ b/solution.py
@@ -329,6 +329,18 @@
     edge = jnp.logical_or(zl == 0, zl == 7)
     beyond = (7 - zl) * 2 + core
 
+    barrier = pltpu.get_barrier_semaphore()
+
+    def signal(sem, peer):
+        pl.semaphore_signal(sem, inc=1, device_id=peer, device_id_type=MESH)
+
+    for peer in reversed(plane_peers):
+        signal(barrier, peer)
+
+    @pl.when(core == 0)
+    def _():
+        signal(barrier, sibling)
+
     loads = [
         pltpu.make_async_copy(pairs_hbm, pairs, in_sem.at[0]),
         pltpu.make_async_copy(field_hbm, fext.at[pl.ds(0, DEPTH)], in_sem.at[1]),
@@ -337,18 +349,6 @@
     ]
     for load in loads:
         load.start()
-
-    barrier = pltpu.get_barrier_semaphore()
-
-    def signal(sem, peer):
-        pl.semaphore_signal(sem, inc=1, device_id=peer, device_id_type=MESH)
-
-    for peer in plane_peers:
-        signal(barrier, peer)
-
-    @pl.when(core == 0)
-    def _():
-        signal(barrier, sibling)
 
     signal(barrier, (zl * 2, (1 - zh) * 16 + here))
     for k in range(1, 8):
@@ -491,11 +491,12 @@
     for _, to, _, put, k in UPWARD + DOWNWARD:
         block = cext.at[put + core]
         send(block, block, swap_sem.at[k], sibling, slab == to)
-    for step in (3, 2, 1):
+    for step in (4, 3, 2, 1):
         z = jnp.where(zl == 0, step, 7 - step)
+        serves = edge if step < 3 else zl == 7
         for _, to, _, put, k in UPWARD + DOWNWARD:
             block = cext.at[put + core]
-            send(block, block, cross_sem.at[k], (z * 2 + core, slab), jnp.logical_and(edge, slab == to))
+            send(block, block, cross_sem.at[k], (z * 2 + core, slab), jnp.logical_and(serves, slab == to))
     for _, to, _, put, k in UPWARD + DOWNWARD:
 
         @pl.when(slab == to)
@@ -534,22 +535,21 @@
     half = jnp.sum(jnp.sum(0.5 * res * res, axis=0, keepdims=True), axis=1, keepdims=True)
     mis[...] = jnp.broadcast_to(half, (1, NX))
     recv_mis[src] = mis[...]
+
+    solve(coef, diag, invd, cinv, resid, direct, work, pe, lam)
+
+    @pl.when(slab < 31)
+    def _():
+        arrived(top, halo_sem.at[4])
+
+    field_terms(fext, hu, slab, DEPTH - 1, DEPTH)
+    cell_products(lam, hu, chunks)
+
     for z in range(8):
         for c in (1, 0):
-            send(mis, recv_mis.at[src], mis_sem, (z * 2 + c, slab), src != z * 2 + c)
-
-    solve(coef, diag, invd, cinv, resid, direct, work, pe, lam)
-
-    @pl.when(slab < 31)
-    def _():
-        arrived(top, halo_sem.at[4])
-
-    field_terms(fext, hu, slab, DEPTH - 1, DEPTH)
-    cell_products(lam, hu, chunks)
-
-    for z in range(8):
-        for c in (1, 0):
-            send(chunks.at[c, z], recv_src.at[src], src_sem, (z * 2 + c, slab), src != z * 2 + c)
+            other = src != z * 2 + c
+            send(chunks.at[c, z], recv_src.at[src], src_sem, (z * 2 + c, slab), other)
+            send(mis, recv_mis.at[src], mis_sem, (z * 2 + c, slab), other)
     recv_src[src] = chunks[core, zl]
     arrived(recv_mis.at[pl.ds(0, 15)], mis_sem)
     arrived(recv_src.at[pl.ds(0, 15)], src_sem)

time: 36.7 us -> 36.4 us (level)
  no operation moved by 1% of the time
where the time goes in v10:
time: 36.4 us; the launch traced here: 36.2 us
  Pallas kernels  35.6 us (98%)
  between operations  0.64 us (2%)
    pallas_call x1, Pallas kernels, on_device(): pl.pallas_call(kernel, name='adjoint_gradient', out_shape=(jax.ShapeDtype...  35 us

profile of v10, /device:TPU:1, one launch (start us, length us, event | category | flops | bytes accessed | tf_op | source)
XLA Modules:
  0.0 36.2 jit_solution(3569321637829094256)
XLA Ops:
  0.6 35.0 %adjoint_gradient.1 = (f32[16,8,128]{2,1,0:T(8,128)S(1)}, f32[16,1,128]{2,1,0:T(1,128)S(1)}) custom-call(f32[4,32,128]{2,1,0:T(8,128)} %cond_hbm.1, f32[4,32,128]{2,1,0:T(8,128)} %bitcast.7, s32[2,2000]{1,0:T(2,128)} %bitcast.8, f32[16,2000]{1,0:T(8,128)} %obs_hbm.1), custom_call_target="tpu_custom_call" | custom-call | tf_op jit(solution)/shard_map/adjoint_gradient/pallas_call | solution.py:587
  35.6 0.6 %add_groups.1 = (f32[8,128]{1,0:T(8,128)}, f32[1,128]{1,0:T(1,128)}) custom-call(f32[16,8,128]{2,1,0:T(8,128)S(1)} %get-tuple-element.6.recv_src, f32[16,1,128]{2,1,0:T(1,128)S(1)} %get-tuple-element.7.recv_mis), custom_call_target="tpu_custom_call" | custom-call | tf_op jit(solution)/shard_map/add_groups/pallas_call | solution.py:631

commit v11 on v10

--- a/solution.py
+++ b/solution.py
@@ -521,6 +521,15 @@
     conductivity_terms(cext, coef, diag, invd, cinv, slab)
     field_terms(fext, hu, slab, 0, DEPTH - 1)
 
+    @pl.when(jnp.logical_not(among(15, 31)))
+    def _():
+        arrived(top, halo_sem.at[4])
+
+    @pl.when(slab != 15)
+    def _():
+        field_terms(fext, hu, slab, DEPTH - 1, DEPTH)
+
+
     @pl.when(core == 0)
     def _():
         arrived(zsum.at[0], z_sem.at[0])
@@ -538,11 +547,11 @@
 
     solve(coef, diag, invd, cinv, resid, direct, work, pe, lam)
 
-    @pl.when(slab < 31)
+    @pl.when(slab == 15)
     def _():
         arrived(top, halo_sem.at[4])
-
-    field_terms(fext, hu, slab, DEPTH - 1, DEPTH)
+        field_terms(fext, hu, slab, DEPTH - 1, DEPTH)
+
     cell_products(lam, hu, chunks)
 
     for z in range(8):

time: 36.4 us -> 36.4 us (level)
  no operation moved by 1% of the time
where the time goes in v11:
time: 36.4 us; the launch traced here: 36.2 us
  Pallas kernels  35.6 us (98%)
  between operations  0.64 us (2%)
    pallas_call x1, Pallas kernels, on_device(): pl.pallas_call(kernel, name='adjoint_gradient', out_shape=(jax.ShapeDtype...  34.9 us

profile of v11, /device:TPU:1, one launch (start us, length us, event | category | flops | bytes accessed | tf_op | source)
XLA Modules:
  0.0 36.2 jit_solution(15550042261733803583)
XLA Ops:
  0.6 34.9 %adjoint_gradient.1 = (f32[16,8,128]{2,1,0:T(8,128)S(1)}, f32[16,1,128]{2,1,0:T(1,128)S(1)}) custom-call(f32[4,32,128]{2,1,0:T(8,128)} %cond_hbm.1, f32[4,32,128]{2,1,0:T(8,128)} %bitcast.7, s32[2,2000]{1,0:T(2,128)} %bitcast.8, f32[16,2000]{1,0:T(8,128)} %obs_hbm.1), custom_call_target="tpu_custom_call" | custom-call | tf_op jit(solution)/shard_map/adjoint_gradient/pallas_call | solution.py:596
  35.6 0.6 %add_groups.1 = (f32[8,128]{1,0:T(8,128)}, f32[1,128]{1,0:T(1,128)}) custom-call(f32[16,8,128]{2,1,0:T(8,128)S(1)} %get-tuple-element.6.recv_src, f32[16,1,128]{2,1,0:T(1,128)S(1)} %get-tuple-element.7.recv_mis), custom_call_target="tpu_custom_call" | custom-call | tf_op jit(solution)/shard_map/add_groups/pallas_call | solution.py:640
